TPU v7x, 32 devices: a whole 2x2x4 slice. The times are simulated.
32 devices in a mesh: dp: 8 (over y, x, core), seq: 4 (over z).
Axes of the slice: x: 2, y: 2, z: 4, core: 2. Of those that a mesh axis runs over, the one named last changes fastest.
Arguments:
- inputs: bfloat16 [8, 1024, 768], P('dp', 'seq'), may hold values from -6 to 6
- cotangent: bfloat16 [8, 1024, 768], P('dp', 'seq'), may hold values from -6 to 6
- norm1_gain: bfloat16 [2, 768], P(None, ('dp', 'seq')), may hold values from 0.5 to 1.5
- norm1_shift: bfloat16 [2, 768], P(None, ('dp', 'seq')), may hold values from -3 to 3
- query_weight: bfloat16 [2, 768, 768], P(None, ('dp', 'seq')), may hold values from -0.21875 to 0.21875
- query_bias: bfloat16 [2, 768], P(None, ('dp', 'seq')), may hold values from -3 to 3
- key_weight: bfloat16 [2, 768, 768], P(None, ('dp', 'seq')), may hold values from -0.21875 to 0.21875
- value_weight: bfloat16 [2, 768, 768], P(None, ('dp', 'seq')), may hold values from -0.21875 to 0.21875
- value_bias: bfloat16 [2, 768], P(None, ('dp', 'seq')), may hold values from -0.75 to 0.75
- out_weight: bfloat16 [2, 768, 768], P(None, ('dp', 'seq')), may hold values from -3.5 to 3.5
- out_bias: bfloat16 [2, 768], P(None, ('dp', 'seq')), may hold values from -3 to 3
- norm2_gain: bfloat16 [2, 768], P(None, ('dp', 'seq')), may hold values from 0.5 to 1.5
- norm2_shift: bfloat16 [2, 768], P(None, ('dp', 'seq')), may hold values from -3 to 3
- hidden_weight: bfloat16 [2, 768, 3072], P(None, ('dp', 'seq')), may hold values from -0.21875 to 0.21875
- hidden_bias: bfloat16 [2, 3072], P(None, ('dp', 'seq')), may hold values from -3 to 3
- proj_weight: bfloat16 [2, 3072, 768], P(None, ('dp', 'seq')), may hold values from -0.109375 to 0.109375
- proj_bias: bfloat16 [2, 768], P(None, ('dp', 'seq')), may hold values from -3 to 3
Outputs:
- outputs: bfloat16 [8, 1024, 768], P('dp', 'seq')
- grad_inputs: float32 [8, 1024, 768], P('dp', 'seq')
- grad_norm1_gain: float32 [2, 768], P(None, ('dp', 'seq'))
- grad_norm1_shift: float32 [2, 768], P(None, ('dp', 'seq'))
- grad_query_weight: float32 [2, 768, 768], P(None, ('dp', 'seq'))
- grad_query_bias: float32 [2, 768], P(None, ('dp', 'seq'))
- grad_key_weight: float32 [2, 768, 768], P(None, ('dp', 'seq'))
- grad_value_weight: float32 [2, 768, 768], P(None, ('dp', 'seq'))
- grad_value_bias: float32 [2, 768], P(None, ('dp', 'seq'))
- grad_out_weight: float32 [2, 768, 768], P(None, ('dp', 'seq'))
- grad_out_bias: float32 [2, 768], P(None, ('dp', 'seq'))
- grad_norm2_gain: float32 [2, 768], P(None, ('dp', 'seq'))
- grad_norm2_shift: float32 [2, 768], P(None, ('dp', 'seq'))
- grad_hidden_weight: float32 [2, 768, 3072], P(None, ('dp', 'seq'))
- grad_hidden_bias: float32 [2, 3072], P(None, ('dp', 'seq'))
- grad_proj_weight: float32 [2, 3072, 768], P(None, ('dp', 'seq'))
- grad_proj_bias: float32 [2, 768], P(None, ('dp', 'seq'))
All inputs are finite; a program needn't handle non-finite values.
Results may differ from a plain program's by a relative error of at most 0.038.
Values may be sent and summed in bfloat16 or wider, within the bound.
No kernel may reach another device: no remote copies, remote signals or barrier semaphores. Data moves between devices by JAX's collectives and lax.ppermute only.
A program may use at most 256 MiB of HBM per device.

v0:
```python
import math

import jax
import jax.numpy as jnp
from jax import lax
from jax.sharding import PartitionSpec as P

HEADS = 12
HEAD_DIM = 64


epsilon = 1e-05


def norm_rows(values, norm_gain, norm_shift):
    center = values - jnp.mean(values, axis=-1, keepdims=True)
    spread = jnp.mean(center * center, axis=-1, keepdims=True)
    return center * lax.rsqrt(spread + epsilon) * norm_gain + norm_shift


def gelu_exact(values):
    return jax.nn.gelu(values, approximate=False)


def linear(left_side, weight):
    return jnp.einsum("ctd,de->cte", left_side, weight, preferred_element_type=jnp.float32)


def linear_back(gradient, weight):
    return jnp.einsum("cte,de->ctd", gradient, weight, preferred_element_type=jnp.float32)


def weight_grad(left_side, gradient):
    return jnp.einsum("ctd,cte->de", left_side, gradient, preferred_element_type=jnp.float32)


def row_total(gradient):
    return jnp.sum(gradient.astype(jnp.float32), axis=(0, 1))


def split_heads(values):
    return values.reshape(values.shape[0], values.shape[1], HEADS, HEAD_DIM)


def fetch_forward(shards, layer_index):
    pieces = [member[layer_index] for member in shards]
    return (
        lax.all_gather(pieces[0], ("dp", "seq"), axis=0, tiled=True),
        lax.all_gather(pieces[1], ("dp", "seq"), axis=0, tiled=True),
        lax.all_gather(pieces[2], ("dp", "seq"), axis=0, tiled=True),
        lax.all_gather(pieces[3], ("dp", "seq"), axis=0, tiled=True),
        lax.all_gather(pieces[4], ("dp", "seq"), axis=0, tiled=True),
        lax.all_gather(pieces[5], ("dp", "seq"), axis=0, tiled=True),
        lax.all_gather(pieces[6], ("dp", "seq"), axis=0, tiled=True),
        lax.all_gather(pieces[7], ("dp", "seq"), axis=0, tiled=True),
        lax.all_gather(pieces[8], ("dp", "seq"), axis=0, tiled=True),
        lax.all_gather(pieces[9], ("dp", "seq"), axis=0, tiled=True),
        lax.all_gather(pieces[10], ("dp", "seq"), axis=0, tiled=True),
        lax.all_gather(pieces[11], ("dp", "seq"), axis=0, tiled=True),
        lax.all_gather(pieces[12], ("dp", "seq"), axis=0, tiled=True),
        lax.all_gather(pieces[13], ("dp", "seq"), axis=0, tiled=True),
        lax.all_gather(pieces[14], ("dp", "seq"), axis=0, tiled=True),
    )


def fetch_backward(shards, layer_index):
    pieces = [member[layer_index] for member in shards]
    return (
        lax.all_gather(pieces[0], ("dp", "seq"), axis=0, tiled=True),
        lax.all_gather(pieces[1], ("dp", "seq"), axis=0, tiled=True),
        lax.all_gather(pieces[2], ("dp", "seq"), axis=0, tiled=True),
        lax.all_gather(pieces[3], ("dp", "seq"), axis=0, tiled=True),
        lax.all_gather(pieces[4], ("dp", "seq"), axis=0, tiled=True),
        lax.all_gather(pieces[5], ("dp", "seq"), axis=0, tiled=True),
        lax.all_gather(pieces[6], ("dp", "seq"), axis=0, tiled=True),
        lax.all_gather(pieces[7], ("dp", "seq"), axis=0, tiled=True),
        lax.all_gather(pieces[8], ("dp", "seq"), axis=0, tiled=True),
        lax.all_gather(pieces[9], ("dp", "seq"), axis=0, tiled=True),
        lax.all_gather(pieces[10], ("dp", "seq"), axis=0, tiled=True),
        lax.all_gather(pieces[11], ("dp", "seq"), axis=0, tiled=True),
        lax.all_gather(pieces[12], ("dp", "seq"), axis=0, tiled=True),
        lax.all_gather(pieces[13], ("dp", "seq"), axis=0, tiled=True),
        lax.all_gather(pieces[14], ("dp", "seq"), axis=0, tiled=True),
    )


def reduce_layer(terms):
    return (
        lax.psum_scatter(terms[0], ("dp", "seq"), scatter_dimension=0, tiled=True),
        lax.psum_scatter(terms[1], ("dp", "seq"), scatter_dimension=0, tiled=True),
        lax.psum_scatter(terms[2], ("dp", "seq"), scatter_dimension=0, tiled=True),
        lax.psum_scatter(terms[3], ("dp", "seq"), scatter_dimension=0, tiled=True),
        lax.psum_scatter(terms[4], ("dp", "seq"), scatter_dimension=0, tiled=True),
        lax.psum_scatter(terms[5], ("dp", "seq"), scatter_dimension=0, tiled=True),
        lax.psum_scatter(terms[6], ("dp", "seq"), scatter_dimension=0, tiled=True),
        lax.psum_scatter(terms[7], ("dp", "seq"), scatter_dimension=0, tiled=True),
        lax.psum_scatter(terms[8], ("dp", "seq"), scatter_dimension=0, tiled=True),
        lax.psum_scatter(terms[9], ("dp", "seq"), scatter_dimension=0, tiled=True),
        lax.psum_scatter(terms[10], ("dp", "seq"), scatter_dimension=0, tiled=True),
        lax.psum_scatter(terms[11], ("dp", "seq"), scatter_dimension=0, tiled=True),
        lax.psum_scatter(terms[12], ("dp", "seq"), scatter_dimension=0, tiled=True),
        lax.psum_scatter(terms[13], ("dp", "seq"), scatter_dimension=0, tiled=True),
        lax.psum_scatter(terms[14], ("dp", "seq"), scatter_dimension=0, tiled=True),
    )


def body(
    inputs,
    cotangent,
    norm1_gain,
    norm1_shift,
    query_weight,
    query_bias,
    key_weight,
    value_weight,
    value_bias,
    out_weight,
    out_bias,
    norm2_gain,
    norm2_shift,
    hidden_weight,
    hidden_bias,
    proj_weight,
    proj_bias,
):
    shards = [
        norm1_gain,
        norm1_shift,
        query_weight,
        query_bias,
        key_weight,
        value_weight,
        value_bias,
        out_weight,
        out_bias,
        norm2_gain,
        norm2_shift,
        hidden_weight,
        hidden_bias,
        proj_weight,
        proj_bias,
    ]
    layer_total = norm1_gain.shape[0]
    scaling = 1.0 / math.sqrt(HEAD_DIM)
    hidden = inputs.astype(jnp.float32)
    saved = []
    for layer_index in range(layer_total):
        weights = fetch_forward(shards, layer_index)
        (
            gain_one,
            shift_one,
            w_query,
            b_query,
            w_key,
            w_value,
            b_value,
            w_out,
            b_out,
            gain_two,
            shift_two,
            w_hidden,
            b_hidden,
            w_proj,
            b_proj,
        ) = weights
        normed_low = norm_rows(
            hidden, gain_one.astype(jnp.float32), shift_one.astype(jnp.float32)
        ).astype(jnp.bfloat16)
        queries = (linear(normed_low, w_query) + b_query.astype(jnp.float32)).astype(jnp.bfloat16)
        key_rows = linear(normed_low, w_key).astype(jnp.bfloat16)
        value_rows = (linear(normed_low, w_value) + b_value.astype(jnp.float32)).astype(
            jnp.bfloat16
        )
        all_keys, all_values = (
            lax.all_gather(key_rows, "seq", axis=1, tiled=True),
            lax.all_gather(value_rows, "seq", axis=1, tiled=True),
        )
        scores = (
            jnp.einsum(
                "cqhe,ckhe->chqk",
                split_heads(queries),
                split_heads(all_keys),
                preferred_element_type=jnp.float32,
            )
            * scaling
        )
        row_max = jnp.max(scores, axis=-1, keepdims=True)
        exponent = jnp.exp(scores - row_max)
        row_sum = jnp.sum(exponent, axis=-1, keepdims=True)
        prob_low = (exponent / row_sum).astype(jnp.bfloat16)
        log_total = row_max + jnp.log(row_sum)
        attended = jnp.einsum(
            "chqk,ckhe->cqhe", prob_low, split_heads(all_values), preferred_element_type=jnp.float32
        )
        attended_low = attended.reshape(hidden.shape).astype(jnp.bfloat16)
        middle = hidden + linear(attended_low, w_out) + b_out.astype(jnp.float32)
        normed_two = norm_rows(
            middle, gain_two.astype(jnp.float32), shift_two.astype(jnp.float32)
        ).astype(jnp.bfloat16)
        preact = linear(normed_two, w_hidden) + b_hidden.astype(jnp.float32)
        active = gelu_exact(preact).astype(jnp.bfloat16)
        following = middle + linear(active, w_proj) + b_proj.astype(jnp.float32)
        stored = None
        saved.append(
            (
                hidden,
                normed_low,
                queries,
                key_rows,
                value_rows,
                log_total,
                attended_low,
                middle,
                normed_two,
                preact,
                active,
                stored,
            )
        )
        hidden = following
    final_output = hidden.astype(jnp.bfloat16)
    upstream = cotangent.astype(jnp.float32)
    collected = []
    for layer_index in reversed(range(layer_total)):
        (
            hidden,
            normed_low,
            queries,
            key_rows,
            value_rows,
            log_total,
            attended_low,
            middle,
            normed_two,
            preact,
            active,
            stored,
        ) = saved[layer_index]
        weights = fetch_backward(shards, layer_index)
        all_keys, all_values = (
            lax.all_gather(key_rows, "seq", axis=1, tiled=True),
            lax.all_gather(value_rows, "seq", axis=1, tiled=True),
        )
        (
            gain_one,
            shift_one,
            w_query,
            b_query,
            w_key,
            w_value,
            b_value,
            w_out,
            b_out,
            gain_two,
            shift_two,
            w_hidden,
            b_hidden,
            w_proj,
            b_proj,
        ) = weights
        grad_low = upstream.astype(jnp.bfloat16)
        grad_proj = weight_grad(active, grad_low)
        grad_pbias = row_total(grad_low)
        grad_active = linear_back(grad_low, w_proj)
        gelu_value, gelu_pull = jax.vjp(gelu_exact, preact)
        grad_pre = gelu_pull(grad_active)[0].astype(jnp.bfloat16)
        grad_hidw = weight_grad(normed_two, grad_pre)
        grad_hbias = row_total(grad_pre)
        grad_normed_two = linear_back(grad_pre, w_hidden)
        norm_value_two, pull_two = jax.vjp(
            norm_rows, middle, gain_two.astype(jnp.float32), shift_two.astype(jnp.float32)
        )
        grad_middle, grad_gain_two, grad_shift_two = pull_two(grad_normed_two)
        grad_mid = upstream + grad_middle
        branch_low = grad_mid.astype(jnp.bfloat16)
        grad_wout = weight_grad(attended_low, branch_low)
        grad_bout = row_total(branch_low)
        grad_att = linear_back(branch_low, w_out).astype(jnp.bfloat16)
        heads_query = split_heads(queries)
        heads_keys = split_heads(all_keys)
        heads_values = split_heads(all_values)
        heads_grad = split_heads(grad_att)
        scores = (
            jnp.einsum(
                "cqhe,ckhe->chqk", heads_query, heads_keys, preferred_element_type=jnp.float32
            )
            * scaling
        )
        probability = jnp.exp(scores - log_total)
        grad_prob_low = jnp.einsum(
            "cqhe,ckhe->chqk", heads_grad, heads_values, preferred_element_type=jnp.float32
        ).astype(jnp.bfloat16)
        inner = jnp.sum(probability * grad_prob_low, axis=-1, keepdims=True)
        grad_scores = (probability * (grad_prob_low - inner)).astype(jnp.bfloat16)
        grad_query = (
            (
                jnp.einsum(
                    "chqk,ckhe->cqhe", grad_scores, heads_keys, preferred_element_type=jnp.float32
                )
                * scaling
            )
            .astype(jnp.bfloat16)
            .reshape(queries.shape)
        )
        prob_low = probability.astype(jnp.bfloat16)
        key_part = (
            jnp.einsum(
                "chqk,cqhe->ckhe", grad_scores, heads_query, preferred_element_type=jnp.float32
            )
            * scaling
        )
        value_part = jnp.einsum(
            "chqk,cqhe->ckhe", prob_low, heads_grad, preferred_element_type=jnp.float32
        )
        key_sum, value_sum = (
            lax.psum_scatter(
                key_part.astype(jnp.bfloat16), "seq", scatter_dimension=1, tiled=True
            ).astype(jnp.float32),
            lax.psum_scatter(
                value_part.astype(jnp.bfloat16), "seq", scatter_dimension=1, tiled=True
            ).astype(jnp.float32),
        )
        grad_key = key_sum.astype(jnp.bfloat16).reshape(key_rows.shape)
        grad_value = value_sum.astype(jnp.bfloat16).reshape(value_rows.shape)
        grad_wq = weight_grad(normed_low, grad_query)
        grad_bq = row_total(grad_query)
        grad_wk = weight_grad(normed_low, grad_key)
        grad_wv = weight_grad(normed_low, grad_value)
        grad_bv = row_total(grad_value)
        grad_normed = (
            linear_back(grad_query, w_query)
            + linear_back(grad_key, w_key)
            + linear_back(grad_value, w_value)
        )
        norm_value_one, pull_one = jax.vjp(
            norm_rows, hidden, gain_one.astype(jnp.float32), shift_one.astype(jnp.float32)
        )
        grad_hidden, grad_gain_one, grad_shift_one = pull_one(grad_normed)
        upstream = grad_mid + grad_hidden
        layer_grads = (
            grad_gain_one,
            grad_shift_one,
            grad_wq,
            grad_bq,
            grad_wk,
            grad_wv,
            grad_bv,
            grad_wout,
            grad_bout,
            grad_gain_two,
            grad_shift_two,
            grad_hidw,
            grad_hbias,
            grad_proj,
            grad_pbias,
        )
        collected.insert(0, reduce_layer(layer_grads))
    stacked = [jnp.stack([entry[member] for entry in collected]) for member in range(15)]
    return (
        final_output,
        upstream,
        stacked[0],
        stacked[1],
        stacked[2],
        stacked[3],
        stacked[4],
        stacked[5],
        stacked[6],
        stacked[7],
        stacked[8],
        stacked[9],
        stacked[10],
        stacked[11],
        stacked[12],
        stacked[13],
        stacked[14],
    )


def solution(mesh):
    return jax.shard_map(
        body,
        mesh=mesh,
        in_specs=(
            P("dp", "seq", None),
            P("dp", "seq", None),
            P(None, ("dp", "seq")),
            P(None, ("dp", "seq")),
            P(None, ("dp", "seq"), None),
            P(None, ("dp", "seq")),
            P(None, ("dp", "seq"), None),
            P(None, ("dp", "seq"), None),
            P(None, ("dp", "seq")),
            P(None, ("dp", "seq"), None),
            P(None, ("dp", "seq")),
            P(None, ("dp", "seq")),
            P(None, ("dp", "seq")),
            P(None, ("dp", "seq"), None),
            P(None, ("dp", "seq")),
            P(None, ("dp", "seq"), None),
            P(None, ("dp", "seq")),
        ),
        out_specs=(
            P("dp", "seq", None),
            P("dp", "seq", None),
            P(None, ("dp", "seq")),
            P(None, ("dp", "seq")),
            P(None, ("dp", "seq"), None),
            P(None, ("dp", "seq")),
            P(None, ("dp", "seq"), None),
            P(None, ("dp", "seq"), None),
            P(None, ("dp", "seq")),
            P(None, ("dp", "seq"), None),
            P(None, ("dp", "seq")),
            P(None, ("dp", "seq")),
            P(None, ("dp", "seq")),
            P(None, ("dp", "seq"), None),
            P(None, ("dp", "seq")),
            P(None, ("dp", "seq"), None),
            P(None, ("dp", "seq")),
        ),
        check_vma=False,
    )
```

profile of v0, /device:TPU:0, one launch (start us, length us, event | category | flops | bytes accessed | tf_op | source)
XLA Modules:
  0.0 2639.7 jit_solution(17637688342624345543)
XLA Ops:
  22.2 43.4 %all-reduce.37 = (bf16[768]{0:T(1024)(128)(2,1)S(1)}, bf16[768]{0:T(1024)(128)(2,1)S(1)}, bf16[768]{0:T(1024)(128)(2,1)S(1)}, bf16[768]{0:T(1024)(128)(2,1)S(1)}...) all-reduce(bf16[768]{0:T(1024)(128)(2,1)S(1)} %dynamic-update-slice, ...), channel_id=5, replica_groups=mesh['dp'=8,'seq'=4] {'dp','seq'}, use_global_device_ids=true, to_apply=%add.2 | all-reduce | flops 18432 | bytes 73728
  71.5 53.3 %all-gather.51.cloned.1.call-done = bf16[1,768,768]{2,1,0:T(8,128)(2,1)} async-done(((bf16[1,24,768]{2,1,0:T(8,128)(2,1)}), bf16[1,768,768]{2,1,0:T(8,128)(2,1)}) %all-gather.51.cloned.1.call-update) | async-done | bytes 1179664 | tf_op jit(solution)/shard_map/all_gather | solution.py:53
  132.0 48.7 %all-gather.55.cloned.1.call-done = bf16[1,768,768]{2,1,0:T(8,128)(2,1)} async-done(((bf16[1,24,768]{2,1,0:T(8,128)(2,1)}), bf16[1,768,768]{2,1,0:T(8,128)(2,1)}) %all-gather.55.cloned.1.call-update) | async-done | bytes 1179664 | tf_op jit(solution)/shard_map/all_gather | solution.py:50
  182.8 36.0 %all-gather.59.cloned.1.call-done = bf16[1024,768]{1,0:T(8,128)(2,1)} async-done(((bf16[256,768]{1,0:T(8,128)(2,1)}), bf16[1024,768]{1,0:T(8,128)(2,1)}) %all-gather.59.cloned.1.call-update) | async-done | bytes 1572880 | tf_op jit(solution)/shard_map/all_gather | solution.py:175
  229.8 26.9 %all-gather.53.cloned.1.call-done = bf16[1024,768]{1,0:T(8,128)(2,1)} async-done(((bf16[256,768]{1,0:T(8,128)(2,1)}), bf16[1024,768]{1,0:T(8,128)(2,1)}) %all-gather.53.cloned.1.call-update) | async-done | bytes 1572880 | tf_op jit(solution)/shard_map/all_gather | solution.py:176
  265.2 47.2 %all-gather.61.cloned.1.call-done = bf16[1,768,768]{2,1,0:T(8,128)(2,1)} async-done(((bf16[1,24,768]{2,1,0:T(8,128)(2,1)}), bf16[1,768,768]{2,1,0:T(8,128)(2,1)}) %all-gather.61.cloned.1.call-update) | async-done | bytes 1179664 | tf_op jit(solution)/shard_map/all_gather | solution.py:55
  314.6 63.7 %all-gather.63.cloned.1.call-done = bf16[1,768,3072]{2,1,0:T(8,128)(2,1)} async-done(((bf16[1,24,3072]{2,1,0:T(8,128)(2,1)}), bf16[1,768,3072]{2,1,0:T(8,128)(2,1)}) %all-gather.63.cloned.1.call-update) | async-done | bytes 4718608 | tf_op jit(solution)/shard_map/all_gather | solution.py:59
  389.7 54.4 %all-gather.65.cloned.1.call-done = bf16[1,3072,768]{2,1,0:T(8,128)(2,1)} async-done(((bf16[1,96,768]{2,1,0:T(8,128)(2,1)}), bf16[1,3072,768]{2,1,0:T(8,128)(2,1)}) %all-gather.65.cloned.1.call-update) | async-done | bytes 4718608 | tf_op jit(solution)/shard_map/all_gather | solution.py:61
  448.4 52.0 %all-gather.67.cloned.1.call-done = bf16[1,768,768]{2,1,0:T(8,128)(2,1)} async-done(((bf16[1,24,768]{2,1,0:T(8,128)(2,1)}), bf16[1,768,768]{2,1,0:T(8,128)(2,1)}) %all-gather.67.cloned.1.call-update) | async-done | bytes 1179664 | tf_op jit(solution)/shard_map/all_gather | solution.py:53
  503.0 53.1 %all-gather.73.cloned.1.call-done = bf16[1,768,768]{2,1,0:T(8,128)(2,1)} async-done(((bf16[1,24,768]{2,1,0:T(8,128)(2,1)}), bf16[1,768,768]{2,1,0:T(8,128)(2,1)}) %all-gather.73.cloned.1.call-update) | async-done | bytes 1179664 | tf_op jit(solution)/shard_map/all_gather | solution.py:52
  562.2 50.3 %all-gather.71.cloned.1.call-done = bf16[1,768,768]{2,1,0:T(8,128)(2,1)} async-done(((bf16[1,24,768]{2,1,0:T(8,128)(2,1)}), bf16[1,768,768]{2,1,0:T(8,128)(2,1)}) %all-gather.71.cloned.1.call-update) | async-done | bytes 1179664 | tf_op jit(solution)/shard_map/all_gather | solution.py:50
  614.5 36.1 %all-gather.69.cloned.1.call-done = bf16[1024,768]{1,0:T(8,128)(2,1)} async-done(((bf16[256,768]{1,0:T(8,128)(2,1)}), bf16[1024,768]{1,0:T(8,128)(2,1)}) %all-gather.69.cloned.1.call-update) | async-done | bytes 1572880 | tf_op jit(solution)/shard_map/all_gather | solution.py:176
  653.2 35.5 %all-gather.75.cloned.1.call-done = bf16[1024,768]{1,0:T(8,128)(2,1)} async-done(((bf16[256,768]{1,0:T(8,128)(2,1)}), bf16[1024,768]{1,0:T(8,128)(2,1)}) %all-gather.75.cloned.1.call-update) | async-done | bytes 1572880 | tf_op jit(solution)/shard_map/all_gather | solution.py:175
  701.4 43.0 %all-gather.77.cloned.1.call-done = bf16[1,768,768]{2,1,0:T(8,128)(2,1)} async-done(((bf16[1,24,768]{2,1,0:T(8,128)(2,1)}), bf16[1,768,768]{2,1,0:T(8,128)(2,1)}) %all-gather.77.cloned.1.call-update) | async-done | bytes 1179664 | tf_op jit(solution)/shard_map/all_gather | solution.py:55
  748.1 62.0 %all-gather.79.cloned.1.call-done = bf16[1,768,3072]{2,1,0:T(8,128)(2,1)} async-done(((bf16[1,24,3072]{2,1,0:T(8,128)(2,1)}), bf16[1,768,3072]{2,1,0:T(8,128)(2,1)}) %all-gather.79.cloned.1.call-update) | async-done | bytes 4718608 | tf_op jit(solution)/shard_map/all_gather | solution.py:59
  822.4 53.4 %all-gather.81.cloned.1.call-done = bf16[1,3072,768]{2,1,0:T(8,128)(2,1)} async-done(((bf16[1,96,768]{2,1,0:T(8,128)(2,1)}), bf16[1,3072,768]{2,1,0:T(8,128)(2,1)}) %all-gather.81.cloned.1.call-update) | async-done | bytes 4718608 | tf_op jit(solution)/shard_map/all_gather | solution.py:61
  926.0 18.7 reduce-scatter.17.cloned.1.call-done
  947.4 33.8 %reduce-scatter.19.cloned.1.call-done = bf16[1,256,12,64]{1,3,2,0:T(8,128)(2,1)} async-done(((bf16[1,1024,12,64]{1,3,2,0:T(8,128)(2,1)}), bf16[1,256,12,64]{1,3,2,0:T(8,128)(2,1)}) %reduce-scatter.19.cloned.1.call-update) | async-done | bytes 393232 | tf_op jit(solution)/shard_map/reduce_scatter | solution.py:319
  1052.8 24.6 reduce-scatter.21.cloned.1.call-done
  1128.3 52.5 %reduce-scatter.39.cloned.1.call-done = f32[24,768]{1,0:T(8,128)} async-done(((f32[768,768]{1,0:T(8,128)}), f32[24,768]{1,0:T(8,128)}) %reduce-scatter.39.cloned.1.call-update) | async-done | bytes 73744 | tf_op jit(solution)/shard_map/reduce_scatter | solution.py:96
  1180.7 104.1 %reduce-scatter.37.cloned.1.call-done = f32[24,768]{1,0:T(8,128)} async-done(((f32[768,768]{1,0:T(8,128)}), f32[24,768]{1,0:T(8,128)}) %reduce-scatter.37.cloned.1.call-update) | async-done | bytes 73744 | tf_op jit(solution)/shard_map/reduce_scatter | solution.py:96
  1286.5 101.8 %reduce-scatter.27.cloned.1.call-done = f32[24,768]{1,0:T(8,128)} async-done(((f32[768,768]{1,0:T(8,128)}), f32[24,768]{1,0:T(8,128)}) %reduce-scatter.27.cloned.1.call-update) | async-done | bytes 73744 | tf_op jit(solution)/shard_map/reduce_scatter | solution.py:91
  1388.3 104.0 %reduce-scatter.25.cloned.1.call-done = f32[24,768]{1,0:T(8,128)} async-done(((f32[768,768]{1,0:T(8,128)}), f32[24,768]{1,0:T(8,128)}) %reduce-scatter.25.cloned.1.call-update) | async-done | bytes 73744 | tf_op jit(solution)/shard_map/reduce_scatter | solution.py:91
  1496.5 152.7 %all-reduce.40.cloned.1.call-done = (f32[768]{0:T(1024)}, f32[768]{0:T(1024)}, f32[768]{0:T(1024)}, f32[768]{0:T(1024)}, f32[768]{0:T(1024)}, /*index=5*/f32[768...) async-done(((f32[768]{0:T(1024)}, f32[768]{0:T(1024)}, ...) | async-done | bytes 73744
  1661.2 93.9 %reduce-scatter.35.cloned.1.call-done = f32[24,768]{1,0:T(8,128)} async-done(((f32[768,768]{1,0:T(8,128)}), f32[24,768]{1,0:T(8,128)}) %reduce-scatter.35.cloned.1.call-update) | async-done | bytes 73744 | tf_op jit(solution)/shard_map/reduce_scatter | solution.py:94
  1755.1 104.1 %reduce-scatter.33.cloned.1.call-done = f32[24,768]{1,0:T(8,128)} async-done(((f32[768,768]{1,0:T(8,128)}), f32[24,768]{1,0:T(8,128)}) %reduce-scatter.33.cloned.1.call-update) | async-done | bytes 73744 | tf_op jit(solution)/shard_map/reduce_scatter | solution.py:94
  1860.8 101.7 %reduce-scatter.31.cloned.1.call-done = f32[24,768]{1,0:T(8,128)} async-done(((f32[768,768]{1,0:T(8,128)}), f32[24,768]{1,0:T(8,128)}) %reduce-scatter.31.cloned.1.call-update) | async-done | bytes 73744 | tf_op jit(solution)/shard_map/reduce_scatter | solution.py:93
  1962.5 104.2 %reduce-scatter.29.cloned.1.call-done = f32[24,768]{1,0:T(8,128)} async-done(((f32[768,768]{1,0:T(8,128)}), f32[24,768]{1,0:T(8,128)}) %reduce-scatter.29.cloned.1.call-update) | async-done | bytes 73744 | tf_op jit(solution)/shard_map/reduce_scatter | solution.py:93
  2068.3 138.9 %reduce-scatter.43.cloned.1.call-done = f32[24,3072]{1,0:T(8,128)} async-done(((f32[768,3072]{1,0:T(8,128)}), f32[24,3072]{1,0:T(8,128)}) %reduce-scatter.43.cloned.1.call-update) | async-done | bytes 294928 | tf_op jit(solution)/shard_map/reduce_scatter | solution.py:100
  2207.2 141.5 %reduce-scatter.41.cloned.1.call-done = f32[24,3072]{1,0:T(8,128)} async-done(((f32[768,3072]{1,0:T(8,128)}), f32[24,3072]{1,0:T(8,128)}) %reduce-scatter.41.cloned.1.call-update) | async-done | bytes 294928 | tf_op jit(solution)/shard_map/reduce_scatter | solution.py:100
  2350.6 138.5 %reduce-scatter.47.cloned.1.call-done = f32[96,768]{1,0:T(8,128)} async-done(((f32[3072,768]{1,0:T(8,128)}), f32[96,768]{1,0:T(8,128)}) %reduce-scatter.47.cloned.1.call-update) | async-done | bytes 294928 | tf_op jit(solution)/shard_map/reduce_scatter | solution.py:102
  2489.1 141.5 %reduce-scatter.45.cloned.1.call-done = f32[96,768]{1,0:T(8,128)} async-done(((f32[3072,768]{1,0:T(8,128)}), f32[96,768]{1,0:T(8,128)}) %reduce-scatter.45.cloned.1.call-update) | async-done | bytes 294928 | tf_op jit(solution)/shard_map/reduce_scatter | solution.py:102
  (478 shorter events, 307.7 us)
Async XLA Ops:
  8.7 116.1 %all-gather.51.cloned.1.call-start = ((), (), s32[]{:S(2)}) async-start(), calls=%async_computation.32 | async-start | bytes 1216512 | tf_op jit(solution)/shard_map/all_gather | solution.py:53
  10.2 170.5 %all-gather.55.cloned.1.call-start = ((), (), s32[]{:S(2)}) async-start(), calls=%async_computation.34 | async-start | bytes 1216512 | tf_op jit(solution)/shard_map/all_gather | solution.py:50
  11.7 207.1 %all-gather.59.cloned.1.call-start = ((), (), s32[]{:S(2)}) async-start(), calls=%async_computation.36 | async-start | bytes 1966080 | tf_op jit(solution)/shard_map/all_gather | solution.py:175
  71.5 185.3 %all-gather.53.cloned.1.call-start = ((), (), s32[]{:S(2)}) async-start(), calls=%async_computation.33 | async-start | bytes 1966080 | tf_op jit(solution)/shard_map/all_gather | solution.py:176
  127.5 185.0 %all-gather.61.cloned.1.call-start = ((), (), s32[]{:S(2)}) async-start(), calls=%async_computation.37 | async-start | bytes 1216512 | tf_op jit(solution)/shard_map/all_gather | solution.py:55
  128.2 250.1 %all-gather.63.cloned.1.call-start = ((), (), s32[]{:S(2)}) async-start(), calls=%async_computation.38 | async-start | bytes 4866048 | tf_op jit(solution)/shard_map/all_gather | solution.py:59
  129.0 315.1 %all-gather.65.cloned.1.call-start = ((), (), s32[]{:S(2)}) async-start(), calls=%async_computation.39 | async-start | bytes 4866048 | tf_op jit(solution)/shard_map/all_gather | solution.py:61
  129.8 370.6 %all-gather.67.cloned.1.call-start = ((), (), s32[]{:S(2)}) async-start(), calls=%async_computation.40 | async-start | bytes 1216512 | tf_op jit(solution)/shard_map/all_gather | solution.py:53
  130.5 425.6 %all-gather.73.cloned.1.call-start = ((), (), s32[]{:S(2)}) async-start(), calls=%async_computation.43 | async-start | bytes 1216512 | tf_op jit(solution)/shard_map/all_gather | solution.py:52
  131.1 481.4 %all-gather.71.cloned.1.call-start = ((), (), s32[]{:S(2)}) async-start(), calls=%async_computation.42 | async-start | bytes 1216512 | tf_op jit(solution)/shard_map/all_gather | solution.py:50
  131.9 518.8 %all-gather.69.cloned.1.call-start = ((), (), s32[]{:S(2)}) async-start(), calls=%async_computation.41 | async-start | bytes 1966080 | tf_op jit(solution)/shard_map/all_gather | solution.py:176
  502.9 185.8 %all-gather.75.cloned.1.call-start = ((), (), s32[]{:S(2)}) async-start(), calls=%async_computation.44 | async-start | bytes 1966080 | tf_op jit(solution)/shard_map/all_gather | solution.py:175
  558.6 185.8 %all-gather.77.cloned.1.call-start = ((), (), s32[]{:S(2)}) async-start(), calls=%async_computation.45 | async-start | bytes 1216512 | tf_op jit(solution)/shard_map/all_gather | solution.py:55
  559.2 250.9 %all-gather.79.cloned.1.call-start = ((), (), s32[]{:S(2)}) async-start(), calls=%async_computation.46 | async-start | bytes 4866048 | tf_op jit(solution)/shard_map/all_gather | solution.py:59
  559.8 316.0 %all-gather.81.cloned.1.call-start = ((), (), s32[]{:S(2)}) async-start(), calls=%async_computation.47 | async-start | bytes 4866048 | tf_op jit(solution)/shard_map/all_gather | solution.py:61
  560.4 384.3 %reduce-scatter.17.cloned.1.call-start = ((), (), s32[]{:S(2)}) async-start(), calls=%async_computation.16 | async-start | bytes 1966080 | tf_op jit(solution)/shard_map/reduce_scatter | solution.py:316
  910.5 70.7 %reduce-scatter.19.cloned.1.call-start = ((), (), s32[]{:S(2)}) async-start(), calls=%async_computation.17 | async-start | bytes 1966080 | tf_op jit(solution)/shard_map/reduce_scatter | solution.py:319
  918.7 132.2 %reduce-scatter.23.cloned.1.call-start = ((), (), s32[]{:S(2)}) async-start(), calls=%async_computation.19 | async-start | bytes 1966080 | tf_op jit(solution)/shard_map/reduce_scatter | solution.py:319
  1006.6 70.8 %reduce-scatter.21.cloned.1.call-start = ((), (), s32[]{:S(2)}) async-start(), calls=%async_computation.18 | async-start | bytes 1966080 | tf_op jit(solution)/shard_map/reduce_scatter | solution.py:316
  1025.6 155.1 %reduce-scatter.39.cloned.1.call-start = ((), (), s32[]{:S(2)}) async-start(), calls=%async_computation.27 | async-start | bytes 2433024 | tf_op jit(solution)/shard_map/reduce_scatter | solution.py:96
  1027.6 257.3 %reduce-scatter.37.cloned.1.call-start = ((), (), s32[]{:S(2)}) async-start(), calls=%async_computation.26 | async-start | bytes 2433024 | tf_op jit(solution)/shard_map/reduce_scatter | solution.py:96
  1029.6 358.7 %reduce-scatter.27.cloned.1.call-start = ((), (), s32[]{:S(2)}) async-start(), calls=%async_computation.21 | async-start | bytes 2433024 | tf_op jit(solution)/shard_map/reduce_scatter | solution.py:91
  1032.8 459.5 %reduce-scatter.25.cloned.1.call-start = ((), (), s32[]{:S(2)}) async-start(), calls=%async_computation.20 | async-start | bytes 2433024 | tf_op jit(solution)/shard_map/reduce_scatter | solution.py:91
  1041.3 607.9 %all-reduce.40.cloned.1.call-start = ((), (), s32[]{:S(2)}) async-start(), calls=%async_computation.48 | async-start | bytes 180224
  1083.7 671.5 %reduce-scatter.35.cloned.1.call-start = ((), (), s32[]{:S(2)}) async-start(), calls=%async_computation.25 | async-start | bytes 2433024 | tf_op jit(solution)/shard_map/reduce_scatter | solution.py:94
  1085.7 773.5 %reduce-scatter.33.cloned.1.call-start = ((), (), s32[]{:S(2)}) async-start(), calls=%async_computation.24 | async-start | bytes 2433024 | tf_op jit(solution)/shard_map/reduce_scatter | solution.py:94
  1088.9 873.6 %reduce-scatter.31.cloned.1.call-start = ((), (), s32[]{:S(2)}) async-start(), calls=%async_computation.23 | async-start | bytes 2433024 | tf_op jit(solution)/shard_map/reduce_scatter | solution.py:93
  1091.0 975.8 %reduce-scatter.29.cloned.1.call-start = ((), (), s32[]{:S(2)}) async-start(), calls=%async_computation.22 | async-start | bytes 2433024 | tf_op jit(solution)/shard_map/reduce_scatter | solution.py:93
  1094.4 1112.8 %reduce-scatter.43.cloned.1.call-start = ((), (), s32[]{:S(2)}) async-start(), calls=%async_computation.29 | async-start | bytes 9732096 | tf_op jit(solution)/shard_map/reduce_scatter | solution.py:100
  1101.2 1247.5 %reduce-scatter.41.cloned.1.call-start = ((), (), s32[]{:S(2)}) async-start(), calls=%async_computation.28 | async-start | bytes 9732096 | tf_op jit(solution)/shard_map/reduce_scatter | solution.py:100
  1108.5 1380.6 %reduce-scatter.47.cloned.1.call-start = ((), (), s32[]{:S(2)}) async-start(), calls=%async_computation.31 | async-start | bytes 9732096 | tf_op jit(solution)/shard_map/reduce_scatter | solution.py:102
  1116.0 1514.6 %reduce-scatter.45.cloned.1.call-start = ((), (), s32[]{:S(2)}) async-start(), calls=%async_computation.30 | async-start | bytes 9732096 | tf_op jit(solution)/shard_map/reduce_scatter | solution.py:102
  (108 other events, 4432.0 us)
Sparse Core Ops, SparseCore 0:
  11.4 57.0 all-gather.56
  71.8 52.9 all-gather.50
  127.7 53.0 all-gather.54
  182.7 36.0 all-gather.58
  220.8 35.9 all-gather.52
  259.4 52.9 all-gather.60
  315.8 62.4 all-gather.62
  381.7 62.3 all-gather.64
  447.5 52.8 all-gather.66
  503.1 53.0 all-gather.72
  559.5 53.0 all-gather.70
  614.6 36.0 all-gather.68
  652.8 35.9 all-gather.74
  691.4 52.9 all-gather.76
  747.6 62.4 all-gather.78
  813.4 62.3 all-gather.80
  946.9 34.2 reduce-scatter.18
  1006.7 34.2 reduce-scatter.22
  1043.1 34.2 reduce-scatter.20
  1082.7 97.9 reduce-scatter.38
  1186.9 97.9 reduce-scatter.36
  1290.2 98.0 reduce-scatter.26
  1394.2 97.9 reduce-scatter.24
  1499.8 149.3 all-reduce.39
  1654.3 100.7 reduce-scatter.34
  1761.1 98.0 reduce-scatter.32
  1864.5 97.9 reduce-scatter.30
  1968.7 98.0 reduce-scatter.28
  2072.5 134.6 reduce-scatter.42
  2214.1 134.5 reduce-scatter.40
  2354.6 134.4 reduce-scatter.46
  2495.8 134.6 reduce-scatter.44
  (1 shorter events, 34.0 us)
where the time goes:
time: 2650 us; the launch traced here: 2640 us
  waiting for transfers between devices  2280 us (86%)
  matrix products  188 us (7%)
  local copies, waits for them, and re-layouts  58.4 us (2%)
  other arithmetic  55.7 us (2%)
  blocking collectives  43.4 us (2%)
    reduce_scatter x2, waiting for transfers between devices, reduce_layer(): lax.psum_scatter(terms[11], ('dp', 'seq'), scatter_dimension=0, tiled=True)  280 us
    reduce_scatter x2, waiting for transfers between devices, reduce_layer(): lax.psum_scatter(terms[13], ('dp', 'seq'), scatter_dimension=0, tiled=True)  280 us
    reduce_scatter x2, waiting for transfers between devices, reduce_layer(): lax.psum_scatter(terms[4], ('dp', 'seq'), scatter_dimension=0, tiled=True)  206 us
    reduce_scatter x2, waiting for transfers between devices, reduce_layer(): lax.psum_scatter(terms[2], ('dp', 'seq'), scatter_dimension=0, tiled=True)  206 us
    reduce_scatter x2, waiting for transfers between devices, reduce_layer(): lax.psum_scatter(terms[5], ('dp', 'seq'), scatter_dimension=0, tiled=True)  198 us
    reduce_scatter x2, waiting for transfers between devices, reduce_layer(): lax.psum_scatter(terms[7], ('dp', 'seq'), scatter_dimension=0, tiled=True)  157 us
    unnamed x34, waiting for transfers between devices  156 us
    all_gather x2, waiting for transfers between devices, fetch_forward(): lax.all_gather(pieces[11], ('dp', 'seq'), axis=0, tiled=True)  126 us
  transfers between devices with their start and end apart: 33, of which 31 were waited for; matrix products, arithmetic and copies ran while one was open for 8% of the time, Pallas kernels for 0%

commit v1 on v0

v1 whole, which is shorter than its diff:
```python
import math

import jax
import jax.numpy as jnp
import numpy as np
from jax import lax
from jax.experimental import pallas as pl
from jax.experimental.pallas import tpu as pltpu
from jax.sharding import PartitionSpec as P

HEADS = 12
HEAD_DIM = 64
PAIRS = HEADS // 2
LANES = 2 * HEAD_DIM
epsilon = 1e-05
SMALL = 128
SUMS = 256
VECTORS = 8
F32 = jnp.float32
BF16 = jnp.bfloat16
BOTH = ("dp", "seq")
SCALE = 1.0 / math.sqrt(HEAD_DIM)
VMEM_BYTES = 62 * 1024 * 1024


def mm(left_side, right_side):
    return lax.dot_general(
        left_side, right_side, (((1,), (0,)), ((), ())), preferred_element_type=F32
    )


def mm_nt(left_side, right_side):
    return lax.dot_general(
        left_side, right_side, (((1,), (1,)), ((), ())), preferred_element_type=F32
    )


def mm_tn(left_side, right_side):
    return lax.dot_general(
        left_side, right_side, (((0,), (0,)), ((), ())), preferred_element_type=F32
    )


def spread_matrix(ways):
    table = np.zeros((128 * ways, 128 * ways), np.float32)
    for source in range(128 * ways):
        table[source, (source % ways) * 128 + source // ways] = 1.0
    return jnp.asarray(table, BF16)


def deinterleave(values, ways):
    rows, columns = values.shape
    groups = columns // (128 * ways)
    moved = mm(values.reshape(rows * groups, 128 * ways), spread_matrix(ways)).astype(values.dtype)
    moved = moved.reshape(rows, groups, ways, 128)
    return moved.transpose(0, 2, 1, 3).reshape(rows, columns)


def norm_parts(values):
    center = values - jnp.mean(values, axis=-1, keepdims=True)
    spread = jnp.mean(center * center, axis=-1, keepdims=True)
    inverse = lax.rsqrt(spread + epsilon)
    return center * inverse, inverse


def norm_rows(values, gain, shift):
    return norm_parts(values)[0] * gain + shift


def norm_back(values, gain, gradient):
    unit, inverse = norm_parts(values)
    scaled = gradient * gain
    mean_plain = jnp.mean(scaled, axis=-1, keepdims=True)
    mean_unit = jnp.mean(scaled * unit, axis=-1, keepdims=True)
    by_values = inverse * (scaled - mean_plain - unit * mean_unit)
    by_gain = jnp.sum(gradient * unit, axis=0, keepdims=True)
    by_shift = jnp.sum(gradient, axis=0, keepdims=True)
    return by_values, by_gain, by_shift


def fetch(source, column, size, target, sem):
    return pltpu.make_async_copy(source.at[:, pl.ds(column, size)], target, sem)


def full(shape, dtype):
    return jax.ShapeDtypeStruct(shape, dtype)


LONG, SHORT = 100.0, 0.05
HINT = [SHORT]


def cost():
    micros = HINT[-1]
    return pl.CostEstimate(
        flops=int(micros * 1.1e9), transcendentals=0, bytes_accessed=int(micros * 3.0e6)
    )


def plain(builder, *operands):
    return builder(*operands)


def long(builder, *operands):
    HINT.append(LONG)
    try:
        return builder(*operands)
    finally:
        HINT.pop()


def call(name, kernel, operands, kept, outs, out_spaces, scratch, ahead):
    vmem = pl.BlockSpec(memory_space=pltpu.VMEM)
    away = pl.BlockSpec(memory_space=pl.ANY)
    ahead = [member for member in ahead if member is not None]
    read = len(operands)

    def used(*refs):
        kernel(*refs[:read], *refs[read + len(ahead) :])

    return pl.pallas_call(
        used,
        name=name,
        cost_estimate=cost(),
        out_shape=outs,
        in_specs=[away if far else vmem for far in kept] + [away] * len(ahead),
        out_specs=[away if far else vmem for far in out_spaces],
        scratch_shapes=scratch,
        compiler_params=pltpu.CompilerParams(vmem_limit_bytes=VMEM_BYTES),
    )(*operands, *ahead)


class Source:
    def __init__(self, arrays, plan=None, block=None):
        self.arrays = arrays
        self.plan = plan
        self.block = block

    def loads(self):
        return 1 if self.plan is None else len(self.plan)

    def load(self, refs, column, size, target, at, sems, first):
        copies = []
        if self.plan is None:
            copies.append(
                pltpu.make_async_copy(
                    refs[0].at[:, pl.ds(column, size)],
                    target.at[:, pl.ds(at, size)],
                    sems.at[first],
                )
            )
        else:
            me = lax.axis_index("dp")
            for number, (array, member, offset, row, count) in enumerate(self.plan):
                start = pl.multiple_of((me ^ offset) * self.block + row, 16)
                rows = refs[array] if member is None else refs[array].at[member]
                copies.append(
                    pltpu.make_async_copy(
                        rows.at[:, pl.ds(column, size)],
                        target.at[pl.ds(start, count), pl.ds(at, size)],
                        sems.at[first + number],
                    )
                )
        for copy in copies:
            copy.start()
        return copies


def wait_all(copies):
    for copy in copies:
        copy.wait()


def forward_qkv(layer, layers, ways, blocks, small, source, small_at, ahead):
    first = layer == 0
    frames, width = blocks[0].shape
    count = len(blocks)
    total = count * frames
    base = layer * (VECTORS + ways)
    sum_rows = -(-layers * (VECTORS + ways) // 8) * 8
    given = [] if first else [small]
    loads = source.loads()
    arrays = len(source.arrays)
    assemble = source.plan is not None

    def kernel(*refs):
        block_refs, refs = refs[:count], refs[count:]
        small_ref = None
        if not first:
            small_ref, *refs = refs
        source_refs, refs = refs[:arrays], refs[arrays:]
        q_out, k_out, v_out, a1_out, *refs = refs
        if first:
            small_ref, *refs = refs
        if assemble:
            weights_hbm, *refs = refs
        weights, sems, out_sem, *refs = refs
        if first:
            narrow = refs[0]
            narrow_copies = source.load(source_refs, small_at, SMALL, narrow, 0, sems, loads)
        copies = source.load(source_refs, 0, 3 * width, weights, 0, sems, 0)
        if first:
            wait_all(narrow_copies)
            small_ref[...] = narrow[...].astype(F32).T[:sum_rows]

        def vector(index):
            return small_ref[base + index : base + index + 1, :]

        for i in range(count):
            block = block_refs[i][...]
            if first:
                block = norm_rows(block.astype(F32), vector(0), vector(1)).astype(BF16)
            a1_out[i * frames : (i + 1) * frames, :] = block
        wait_all(copies)
        if assemble:
            assembled = pltpu.make_async_copy(weights, weights_hbm, out_sem.at[0])
            assembled.start()
        q_out[...] = (mm(a1_out[:frames, :], weights[:, :width]) + vector(2)).astype(BF16)
        k_out[...] = mm(a1_out[...], weights[:, width : 2 * width]).astype(BF16)
        v_out[...] = (mm(a1_out[...], weights[:, 2 * width :]) + vector(3)).astype(BF16)
        if assemble:
            assembled.wait()

    outs = [
        full((frames, width), BF16),
        full((total, width), BF16),
        full((total, width), BF16),
        full((total, width), BF16),
    ]
    spaces = [False] * 4
    scratch = [
        pltpu.VMEM((width, 3 * width), BF16),
        pltpu.SemaphoreType.DMA((2 * loads,)),
        pltpu.SemaphoreType.DMA((1,)),
    ]
    if first:
        outs.append(full((sum_rows, width), F32))
        spaces.append(False)
        scratch.append(pltpu.VMEM((width, SMALL), BF16))
    if assemble:
        outs.append(full((width, 3 * width), BF16))
        spaces.append(True)
    operands = [*blocks, *given, *source.arrays]
    far = [False] * (len(operands) - arrays) + [True] * arrays
    q, k, v, a1_full, *rest = call("forward_qkv", kernel, operands, far, outs, spaces, scratch, ahead)
    if first:
        small, *rest = rest
    return q, k, v, a1_full, small, rest[0] if assemble else source.arrays[0]


def both_heads(rows, low):
    zero = jnp.zeros_like(rows)
    return jnp.concatenate([jnp.where(low, rows, zero), jnp.where(low, zero, rows)], axis=0)


def forward_heads(q, k, v, ahead):
    frames, width = q.shape

    def kernel(q_ref, k_ref, v_ref, lse_out, o_out, lse_ref):
        lane = lax.broadcasted_iota(jnp.int32, (1, LANES), 1)
        low = lane < HEAD_DIM
        lse_ref[...] = jnp.zeros_like(lse_ref)

        def pair(index, carry):
            columns = pl.ds(pl.multiple_of(index * LANES, LANES), LANES)
            k2 = k_ref[:, columns]
            v2 = v_ref[:, columns]
            scores = mm_nt(both_heads(q_ref[:, columns] * SCALE, low), k2)
            top = jnp.max(scores, axis=-1, keepdims=True)
            exponent = jnp.exp(scores - top)
            sums = jnp.sum(exponent, axis=-1, keepdims=True)
            mixed = mm(exponent.astype(BF16), v2) * (1.0 / sums)
            lse_ref[...] = jnp.where(lane == index, top + jnp.log(sums), lse_ref[...])
            o_out[:, columns] = jnp.where(low, mixed[:frames], mixed[frames:]).astype(BF16)
            return carry

        lax.fori_loop(0, PAIRS, pair, 0)
        lse_out[...] = lse_ref[...].T[: lse_out.shape[0]]

    return call(
        "forward_heads",
        kernel,
        [q, k, v],
        [False] * 3,
        [full((8, 2 * frames), F32), full((frames, width), BF16)],
        [False] * 2,
        [pltpu.VMEM((2 * frames, LANES), F32)],
        ahead,
    )


def forward_mlp(layer, last, ways, own, o, small, source, at, ahead):
    frames, width = o.shape
    base = layer * (VECTORS + ways)
    loads = source.loads()
    arrays = len(source.arrays)
    assemble = source.plan is not None
    cuts = (0, (1 + ways) * width, (1 + 2 * ways) * width)

    def kernel(own_ref, o_ref, small_ref, *refs):
        source_refs, refs = refs[:arrays], refs[arrays:]
        h1_out, a2_out, g_out, slope_out, h_out, *refs = refs
        if not last:
            next_out, *refs = refs
        if assemble:
            weights_hbm, *refs = refs
        weights, sems, out_sem = refs
        copies = [
            source.load(
                source_refs,
                at + cuts[part],
                cuts[part + 1] - cuts[part],
                weights,
                cuts[part],
                sems,
                part * loads,
            )
            for part in range(2)
        ]

        def vector(index):
            return small_ref[base + index : base + index + 1, :]

        def weight(index):
            return weights[:, index * width : (index + 1) * width]

        hidden = own_ref[...].astype(F32) + vector(4)
        wait_all(copies[0])
        middle = hidden + mm(o_ref[...], weight(0))
        h1_out[...] = middle
        a2 = norm_rows(middle, vector(5), vector(6)).astype(BF16)
        a2_out[...] = a2
        following = middle + vector(7)
        for b in range(ways):
            u = mm(a2, weight(1 + b)) + vector(VECTORS + b)
            phi = 0.5 + 0.5 * lax.erf(u * math.sqrt(0.5))
            density = jnp.exp(-0.5 * u * u) * (1.0 / math.sqrt(2.0 * math.pi))
            g = (u * phi).astype(BF16)
            g_out[:, b * width : (b + 1) * width] = g
            slope_out[:, b * width : (b + 1) * width] = (phi + u * density).astype(BF16)
            if b == 0:
                wait_all(copies[1])
                if assemble:
                    assembled = pltpu.make_async_copy(weights, weights_hbm, out_sem.at[0])
                    assembled.start()
            following = following + mm(g, weight(1 + ways + b))
        h_out[...] = following.astype(h_out.dtype)
        if not last:
            up = base + VECTORS + ways
            next_out[...] = norm_rows(
                following, small_ref[up : up + 1, :], small_ref[up + 1 : up + 2, :]
            ).astype(BF16)
        if assemble:
            assembled.wait()

    row = (frames, width)
    outs = [
        full(row, F32),
        full(row, BF16),
        full((frames, ways * width), BF16),
        full((frames, ways * width), BF16),
        full(row, BF16 if last else F32),
    ]
    spaces = [False] * 5
    if not last:
        outs.append(full(row, BF16))
        spaces.append(False)
    if assemble:
        outs.append(full((width, cuts[2]), BF16))
        spaces.append(True)
    operands = [own, o, small, *source.arrays]
    h1, a2, g, slope, following, *rest = call(
        "forward_mlp",
        kernel,
        operands,
        [False] * 3 + [True] * arrays,
        outs,
        spaces,
        [
            pltpu.VMEM((width, cuts[2]), BF16),
            pltpu.SemaphoreType.DMA((2 * loads,)),
            pltpu.SemaphoreType.DMA((1,)),
        ],
        ahead,
    )
    a1_next = None
    if not last:
        a1_next, *rest = rest
    weights, weights_at = (rest[0], 0) if assemble else (source.arrays[0], at)
    return h1, a2, g, slope, following, a1_next, weights, weights_at


class Target:
    def __init__(self, width, columns, split):
        self.columns = columns
        self.split = split
        self.outs = [full((width, columns), BF16)]
        self.copies = 1
        if split:
            self.blocks = width // split // 2
            self.outs = [full((self.blocks, split, columns), BF16)] * 2
            self.copies = 2 * self.blocks

    def put(self, terms, refs, start, size, sems, first):
        part = pl.ds(start, size)
        copies = []
        if self.split:
            core = lax.axis_index("dp") & 1
            for which in range(2):
                for block in range(self.blocks):
                    row = pl.multiple_of((2 * block + (core ^ which)) * self.split, 16)
                    copies.append(
                        pltpu.make_async_copy(
                            terms.at[pl.ds(row, self.split), part],
                            refs[which].at[block, :, part],
                            sems.at[first + len(copies)],
                        )
                    )
        else:
            copies.append(
                pltpu.make_async_copy(terms.at[:, part], refs[0].at[:, part], sems.at[first])
            )
        for copy in copies:
            copy.start()
        return copies


def backward_mlp(layer, ways, above, small, sums, h1, a2, g, slope, mlp, mlp_at, split, ahead):
    last = len(above) == 1
    frames, width = h1.shape
    base = layer * (VECTORS + ways)
    up = base + VECTORS + ways
    target = Target(width, 2 * ways * width, split)

    def kernel(*refs):
        above_refs = refs[: len(above)]
        small_ref, sums_ref, h1_ref, a2_ref, g_ref, slope_ref, mlp_hbm = refs[
            len(above) : len(above) + 7
        ]
        refs = refs[len(above) + 7 :]
        target_refs, refs = refs[: len(target.outs)], refs[len(target.outs) :]
        dh1_out, sums_out, w_hidden, w_proj, grads, sems, out_sems = refs
        w_copies = []
        for b in range(ways):
            for part, held in ((1, w_proj), (0, w_hidden)):
                w_copies.append(
                    fetch(
                        mlp_hbm,
                        mlp_at + (part * ways + b) * width,
                        width,
                        held.at[b],
                        sems.at[part * ways + b],
                    )
                )
        for copy in w_copies:
            copy.start()
        sums_out[...] = sums_ref[...]
        if last:
            dh = above_refs[0][...].astype(F32)
        else:
            dh1_above, da1, h_above = above_refs[0], above_refs[1], above_refs[2]
            gradient = da1[...] + above_refs[3][0].astype(F32) + above_refs[4][...].astype(F32)
            part, by_gain, by_shift = norm_back(
                h_above[...], small_ref[up : up + 1, :], gradient
            )
            dh = dh1_above[...] + part
            sums_out[up : up + 1, :] = by_gain
            sums_out[up + 1 : up + 2, :] = by_shift
        dm = dh.astype(BF16)
        sums_out[base + 7 : base + 8, :] = jnp.sum(dm.astype(F32), axis=0, keepdims=True)
        a2_turned = a2_ref[...].T
        da2 = jnp.zeros((frames, width), F32)
        out_copies = []

        def put(index):
            out_copies.extend(
                target.put(
                    grads, target_refs, index * width, 2 * width, out_sems, len(out_copies)
                )
            )

        for b in range(ways):
            part = slice(b * width, (b + 1) * width)
            w_copies[2 * b].wait()
            dg = mm_nt(dm, w_proj[b])
            du = (dg * slope_ref[:, part].astype(F32)).astype(BF16)
            sums_out[base + VECTORS + b : base + VECTORS + b + 1, :] = jnp.sum(
                du.astype(F32), axis=0, keepdims=True
            )
            w_copies[2 * b + 1].wait()
            da2 = da2 + mm_nt(du, w_hidden[b])
            grads[:, part] = mm(a2_turned, du).astype(BF16)
            grads[:, (ways + b) * width : (ways + b + 1) * width] = mm_tn(
                g_ref[:, part], dm
            ).astype(BF16)
            if b % 2:
                put(b - 1)
                put(ways + b - 1)
        part, by_gain, by_shift = norm_back(h1_ref[...], small_ref[base + 5 : base + 6, :], da2)
        dh1_out[...] = dh + part
        sums_out[base + 5 : base + 6, :] = by_gain
        sums_out[base + 6 : base + 7, :] = by_shift
        wait_all(out_copies)

    operands = [*above, small, sums, h1, a2, g, slope, mlp]
    result = call(
        "backward_mlp",
        kernel,
        operands,
        [False] * (len(operands) - 1) + [True],
        target.outs + [full((frames, width), F32), full(sums.shape, F32)],
        [True] * len(target.outs) + [False, False],
        [
            pltpu.VMEM((ways, width, width), BF16),
            pltpu.VMEM((ways, width, width), BF16),
            pltpu.VMEM((width, 2 * ways * width), BF16),
            pltpu.SemaphoreType.DMA((2 * ways,)),
            pltpu.SemaphoreType.DMA((ways * target.copies,)),
        ],
        ahead,
    )
    return result[:-2], result[-2], result[-1]


def backward_attention(
    layer, ways, given, q, k, v, lse, raw, small, sums, w_qkv, w_out, out_at, pairs, before, ahead
):
    frames, width = q.shape
    total = k.shape[0]
    count = total // frames
    base = layer * (VECTORS + ways)
    start, stop = pairs
    opening = start == 0
    closing = stop == PAIRS
    columns_out = (stop - start) * LANES
    cuts = len(before) + 1

    def kernel(given_ref, q_ref, k_ref, v_ref, lse_ref, sums_ref, *refs):
        if opening:
            out_hbm, *refs = refs
        if closing:
            earlier, refs = refs[: 3 * (cuts - 1)], refs[3 * (cuts - 1) :]
            raw_refs, refs = refs[: len(raw)], refs[len(raw) :]
            qkv_hbm, *refs = refs
        dq_out, dk_out, dv_out, sums_out, *refs = refs
        sums_out[...] = sums_ref[...]
        if opening:
            dz_out, do_ref, *refs = refs
        else:
            do_ref = given_ref
        if closing:
            da_outs, refs = refs[:3], refs[3:]
            da_own, da_pair, da_cross = da_outs
            da_outs = [da_own, da_pair.at[0], da_cross, da_pair.at[1]]
        if opening:
            w_out_ref, sem, *refs = refs
            copy = fetch(out_hbm, out_at, width, w_out_ref, sem.at[0])
            copy.start()
        if closing:
            weights, sems, dq_all, dk_all, dv_all = refs
            copies = [
                fetch(qkv_hbm, i * width, width, weights.at[i], sems.at[i]) for i in range(3)
            ]
            for i in (1, 2, 0):
                copies[i].start()
        if opening:
            dz = given_ref[...].astype(BF16)
            dz_out[...] = dz
            sums_out[base + 4 : base + 5, :] = jnp.sum(dz.astype(F32), axis=0, keepdims=True)
            copy.wait()
            do_ref[...] = mm_nt(dz, w_out_ref[...]).astype(BF16)
        low = lax.broadcasted_iota(jnp.int32, (1, LANES), 1) < HEAD_DIM
        low_rows = lax.broadcasted_iota(jnp.int32, (LANES, 1), 0) < HEAD_DIM

        def pair(index, carry):
            columns = pl.ds(pl.multiple_of(index * LANES, LANES), LANES)
            target = pl.ds(pl.multiple_of((index - start) * LANES, LANES), LANES)
            q4 = both_heads(q_ref[:, columns] * SCALE, low)
            do4 = both_heads(do_ref[:, columns], low)
            k2 = k_ref[:, columns]
            p = jnp.exp(mm_nt(k2, q4) - lse_ref[pl.ds(index, 1), :])
            share = p * mm_nt(v_ref[:, columns], do4)
            inner = jnp.sum(share, axis=0, keepdims=True)
            ds = (share - p * inner).astype(BF16)
            dv2 = mm(p.astype(BF16), do4).astype(BF16)
            dk2 = mm(ds, q4).astype(BF16)
            turned = mm_tn(k2, ds)
            dq2 = jnp.where(low_rows, turned[:, :frames], turned[:, frames:]).T * SCALE
            dq_out[:, target] = dq2.astype(BF16)
            dk_out[:, target] = dk2
            dv_out[:, target] = dv2
            return carry

        lax.fori_loop(start, stop, pair, 0)
        if not closing:
            return
        at = 0
        for number in range(cuts):
            if number < cuts - 1:
                members = earlier[3 * number : 3 * number + 3]
            else:
                members = (dq_out, dk_out, dv_out)
            size = members[0].shape[1]
            for member, whole in zip(members, (dq_all, dk_all, dv_all)):
                whole[:, at : at + size] = member[...]
            at += size
        wait_all(copies)
        for i in range(count):
            rows = slice(i * frames, (i + 1) * frames)
            da = mm_nt(dk_all[rows, :], weights[1]) + mm_nt(dv_all[rows, :], weights[2])
            if i == 0:
                da = da + mm_nt(dq_all[...], weights[0])
                by_gain = jnp.zeros((1, width), F32)
                by_shift = jnp.zeros((1, width), F32)
            if raw:
                unit, _ = norm_parts(raw_refs[i][...].astype(F32))
                by_gain += jnp.sum(da * unit, axis=0, keepdims=True)
                by_shift += jnp.sum(da, axis=0, keepdims=True)
            da_outs[i][...] = da.astype(da_outs[i].dtype)
        if raw:
            sums_out[base : base + 1, :] = by_gain
            sums_out[base + 1 : base + 2, :] = by_shift
        sums_out[base + 2 : base + 3, :] = jnp.sum(dq_all[...].astype(F32), axis=0, keepdims=True)
        sums_out[base + 3 : base + 4, :] = jnp.sum(dv_all[...].astype(F32), axis=0, keepdims=True)

    row = (frames, width)
    outs = [
        full((frames, columns_out), BF16),
        full((total, columns_out), BF16),
        full((total, columns_out), BF16),
        full(sums.shape, F32),
    ]
    operands = [given, q, k, v, lse, sums]
    far = [False] * 6
    scratch = []
    if opening:
        outs += [full(row, BF16), full(row, BF16)]
        operands.append(w_out)
        far.append(True)
        scratch += [pltpu.VMEM((width, width), BF16), pltpu.SemaphoreType.DMA((1,))]
    if closing:
        outs += [full(row, F32), full((2,) + row, BF16), full(row, BF16)]
        extra = [member for part in before for member in part] + list(raw)
        operands += [*extra, w_qkv]
        far += [False] * len(extra) + [True]
        scratch += [
            pltpu.VMEM((3, width, width), BF16),
            pltpu.SemaphoreType.DMA((3,)),
            pltpu.VMEM(row, BF16),
            pltpu.VMEM((total, width), BF16),
            pltpu.VMEM((total, width), BF16),
        ]
    result = call(
        "backward_attention", kernel, operands, far, outs, [False] * len(outs), scratch, ahead
    )
    parts, sums, rest = list(result[:3]), result[3], list(result[4:])
    opened, rest = (rest[:2], rest[2:]) if opening else ([], rest)
    return parts, sums, opened, rest


def attention_grads(a1, o, dz, parts, sums, split, ahead):
    total, width = a1.shape
    frames = o.shape[0]
    columns = 4 * width + (SUMS if sums is not None else 0)
    extra = [] if sums is None else [sums]
    target = Target(width, columns, split)
    cuts = len(parts)

    def kernel(a1_ref, o_ref, dz_ref, *refs):
        part_refs, refs = refs[: 3 * cuts], refs[3 * cuts :]
        if extra:
            sums_ref, *refs = refs
        target_refs, refs = refs[: len(target.outs)], refs[len(target.outs) :]
        grads, turned, sems = refs
        copies = []

        def put(start, size):
            copies.extend(target.put(grads, target_refs, start, size, sems, len(copies)))

        if extra:
            table = sums_ref[...]
            table = jnp.concatenate(
                [table, jnp.zeros((128 - table.shape[0], width), F32)], axis=0
            )
            grads[:, 4 * width : 4 * width + 128] = table.T.astype(BF16)
            grads[:, 4 * width + 128 : columns] = jnp.zeros((width, SUMS - 128), BF16)
        grads[:, 3 * width : 4 * width] = mm(o_ref[...].T, dz_ref[...]).astype(BF16)
        put(3 * width, columns - 3 * width)
        turned[...] = a1_ref[...].T
        for index in range(3):
            column = index * width
            for number in range(cuts):
                ref = part_refs[3 * number + index]
                size = ref.shape[1]
                left = turned[:, :frames] if index == 0 else turned[...]
                grads[:, column : column + size] = mm(left, ref[...]).astype(BF16)
                column += size
            if index:
                put((0, 0, 2 * width)[index], (0, 2 * width, width)[index])
        wait_all(copies)

    operands = [a1, o, dz, *(member for part in parts for member in part), *extra]
    return call(
        "attention_grads",
        kernel,
        operands,
        [False] * len(operands),
        target.outs,
        [True] * len(target.outs),
        [
            pltpu.VMEM((width, columns), BF16),
            pltpu.VMEM((width, total), BF16),
            pltpu.SemaphoreType.DMA((3 * target.copies,)),
        ],
        ahead,
    )


def finish_rows(raw, dh1, small, parts, ahead):
    frames, width = dh1.shape

    def kernel(raw_ref, dh1_ref, small_ref, *refs):
        gradient = refs[0][...] + refs[1][0].astype(F32) + refs[2][...].astype(F32)
        part, _, _ = norm_back(raw_ref[...].astype(F32), small_ref[0:1, :], gradient)
        refs[-1][...] = (dh1_ref[...] + part).astype(BF16)

    operands = [raw, dh1, small, *parts]
    return call(
        "finish_rows",
        kernel,
        operands,
        [False] * len(operands),
        [full((frames, width), BF16)],
        [False],
        [],
        ahead,
    )[0]


def hold(values, column, columns, ahead):
    def kernel(source, target):
        target[...] = source[:, column : column + columns]

    outs = [full((values.shape[0], columns), values.dtype)]
    return call("hold", kernel, [values], [False], outs, [False], [], ahead)[0]


def join(members, ahead):
    count = len(members)

    def kernel(*refs):
        for index in range(count):
            refs[count][index] = refs[index][...]

    outs = [full((count,) + members[0].shape, members[0].dtype)]
    return call("join", kernel, members, [False] * count, outs, [False], [], ahead)[0]


def relay(base, first, second, ahead):
    rows, width = base.shape
    half = rows // 2

    def kernel(base_ref, first_ref, second_ref, upper_out, lower_out, joined):
        upper_out[...] = second_ref[:half, :]
        lower_out[...] = first_ref[half:, :]
        for index, ref in enumerate((base_ref, first_ref, second_ref)):
            joined[index] = ref[...]

    outs = [full((half, width), BF16)] * 2 + [full((3, rows, width), BF16)]
    return call(
        "relay", kernel, [base, first, second], [False] * 3, outs, [False] * 3, [], ahead
    )


def assemble(members, ahead):
    rows, width = members[0].shape
    count = len(members)

    def kernel(*refs):
        position = lax.axis_index("seq")
        for step in range(count):
            refs[count][position ^ step] = refs[step][...]

    outs = [full((count, rows, width), members[0].dtype)]
    whole = call("assemble", kernel, members, [False] * count, outs, [False], [], ahead)[0]
    return whole.reshape(count * rows, width)


def column_block(columns):
    for size in range(1664, 0, -128):
        if columns % size == 0:
            return size
    return columns


def add_halves(bits, kept, received, stage, ahead):
    if stage == 1:
        blocks, rows, columns = kept[0].shape
        cut = columns // 2
        lead = blocks // 2
    else:
        blocks, rows, cut = kept[0].shape
        lead = blocks // 2
    size = column_block(cut)
    steps = cut // size

    def where(right, sent):
        def index(block, column, own):
            x, y = own[1] ^ int(sent), own[2] ^ int(sent)
            if stage == 1:
                if right:
                    return (2 * y + block, 0, column + steps)
                return (2 * block + x, 0, column)
            return (x if right else y, 0, column)

        return index

    operands, in_specs = [], []
    for right in (False, True):
        for sent in (False, True):
            source = 0 if stage == 1 else int(right)
            for member in (kept[source], received[source]):
                operands.append(member)
                in_specs.append(pl.BlockSpec((1, rows, size), where(right, sent)))

    ahead = [member for member in ahead if member is not None]

    def kernel(own, *refs):
        outs = refs[8 + len(ahead) :]
        for number in range(4):
            outs[number][...] = (
                refs[2 * number][...].astype(F32) + refs[2 * number + 1][...].astype(F32)
            ).astype(BF16)

    out_spec = pl.BlockSpec((1, rows, size), lambda block, column, own: (block, 0, column))
    return pl.pallas_call(
        kernel,
        name="add_halves",
        cost_estimate=cost(),
        out_shape=[full((lead, rows, cut), BF16)] * 4,
        grid_spec=pltpu.PrefetchScalarGridSpec(
            num_scalar_prefetch=1,
            grid=(lead, steps),
            in_specs=in_specs + [pl.BlockSpec(memory_space=pl.ANY)] * len(ahead),
            out_specs=[out_spec] * 4,
        ),
        compiler_params=pltpu.CompilerParams(vmem_limit_bytes=VMEM_BYTES),
    )(bits, *operands, *ahead)


def add_rows(kept, received, parts, ahead):
    _, block, half = kept[0].shape
    rows = block // parts
    width = 2 * half

    def kernel(left, left_in, right, right_in, mine_out, other_out, total):
        total[:, :half] = left[0].astype(F32) + left_in[0].astype(F32)
        total[:, half:] = right[0].astype(F32) + right_in[0].astype(F32)
        low = lax.axis_index("seq") & 1
        for index in range(parts // 2):
            for out, which in ((mine_out, low), (other_out, 1 - low)):
                start = pl.multiple_of((2 * index + which) * rows, 8)
                out[index] = total[pl.ds(start, rows), :].astype(BF16)

    return call(
        "add_rows",
        kernel,
        [kept[0], received[0], kept[1], received[1]],
        [False] * 4,
        [full((parts // 2, rows, width), BF16)] * 2,
        [False] * 2,
        [pltpu.VMEM((block, width), F32)],
        ahead,
    )


def add_block(kept, received, ahead):
    _, block, half = kept[0].shape

    def kernel(left, left_in, right, right_in, out):
        out[:, :half] = (left[0].astype(F32) + left_in[0].astype(F32)).astype(BF16)
        out[:, half:] = (right[0].astype(F32) + right_in[0].astype(F32)).astype(BF16)

    operands = [kept[0], received[0], kept[1], received[1]]
    outs = [full((block, 2 * half), BF16)]
    return call("add_block", kernel, operands, [False] * 4, outs, [False], [], ahead)[0]


def add_ends(kept, received, ahead):
    _, rows, width = kept.shape

    def kernel(kept_ref, received_ref, mine_out, other_out):
        high = lax.axis_index("seq") >> 1
        for out, which in ((mine_out, high), (other_out, 1 - high)):
            out[...] = (
                kept_ref[which].astype(F32) + received_ref[which].astype(F32)
            ).astype(BF16)

    return call(
        "add_ends",
        kernel,
        [kept, received],
        [False] * 2,
        [full((rows, width), BF16)] * 2,
        [False] * 2,
        [],
        ahead,
    )


def add_cross(kept, received, ahead):
    def kernel(kept_ref, received_ref, out):
        out[...] = (kept_ref[...].astype(F32) + received_ref[1].astype(F32)).astype(BF16)

    outs = [full(kept.shape, BF16)]
    return call(
        "add_cross", kernel, [kept, received], [False] * 2, outs, [False], [], ahead
    )[0]


def add_parts(members, ahead):
    def kernel(*refs):
        refs[-1][...] = total_of(refs[:-1], slice(None))

    outs = [full(members[0].shape, F32)]
    return call("add_parts", kernel, members, [False] * len(members), outs, [False], [], ahead)[0]


def total_of(refs, columns):
    value = refs[0][:, columns].astype(F32)
    for ref in refs[1:]:
        value = value + ref[:, columns].astype(F32)
    return value


def finish_mlp(layers, table, ways, ahead):
    rows, columns = layers[0][0].shape
    half = columns // 2
    counts = [len(members) for members in layers]
    width = half // ways

    def kernel(table_ref, *refs):
        hidden_out, proj_out = refs[sum(counts) :]
        row = lax.broadcasted_iota(jnp.int32, (rows * ways, rows * ways), 0)
        column = lax.broadcasted_iota(jnp.int32, (rows * ways, rows * ways), 1)
        turn = jnp.where(row == ways * (column % rows) + column // rows, 1.0, 0.0).astype(BF16)
        at = 0
        for layer, count in enumerate(counts):
            members = refs[at : at + count]
            at += count
            proj = jnp.concatenate(
                [
                    total_of(members, slice(half + b * width, half + (b + 1) * width))
                    for b in range(ways)
                ],
                axis=0,
            )
            proj_out[layer] = mm(turn, proj.astype(BF16))
            hidden = total_of(members, slice(0, half)).astype(BF16)
            for start in range(0, width, 128):
                group = jnp.concatenate(
                    [hidden[:, b * width + start : b * width + start + 128] for b in range(ways)],
                    axis=1,
                )
                hidden_out[layer, :, ways * start : ways * (start + 128)] = mm_nt(
                    group, table_ref[...]
                )

    operands = [table] + [member for members in layers for member in members]
    outs = [
        full((len(layers), rows, half), F32),
        full((len(layers), rows * ways, width), F32),
    ]
    return call(
        "finish_mlp", kernel, operands, [False] * len(operands), outs, [False] * 2, [], ahead
    )


def finish_attention(layers, ways, ahead):
    rows, columns = layers[0][0].shape
    counts = [len(members) for members in layers]
    width = (columns - SUMS) // 4
    each = VECTORS + ways

    def kernel(*refs):
        outs = refs[sum(counts) :]
        at = 0
        for layer, count in enumerate(counts):
            members = refs[at : at + count]
            at += count
            for index in range(4):
                outs[index][layer] = total_of(
                    members, slice(index * width, (index + 1) * width)
                )
            if layer == 0:
                sums = total_of(members, slice(4 * width, 4 * width + 128)).T
        for layer in range(len(counts)):
            for index in range(VECTORS):
                row = layer * each + index
                outs[4 + index][layer : layer + 1, :] = sums[row : row + 1, :]
            row = layer * each + VECTORS
            outs[4 + VECTORS][layer] = sums[row : row + ways, :]

    operands = [member for members in layers for member in members]
    count = len(layers)
    outs = [full((count, rows, width), F32)] * 4 + [full((count, rows), F32)] * VECTORS
    outs.append(full((count, ways, rows), F32))
    result = call(
        "finish_attention",
        kernel,
        operands,
        [False] * len(operands),
        outs,
        [False] * len(outs),
        [],
        ahead,
    )
    return result[:4], result[4:-1], result[-1]


def body(inputs, cotangent, *parameters):
    (
        norm1_gain,
        norm1_shift,
        query_weight,
        query_bias,
        key_weight,
        value_weight,
        value_bias,
        out_weight,
        out_bias,
        norm2_gain,
        norm2_shift,
        hidden_weight,
        hidden_bias,
        proj_weight,
        proj_bias,
    ) = parameters
    layers, rows, width = query_weight.shape
    ways = proj_weight.shape[1] // rows
    frames = inputs.shape[1]
    groups = lax.axis_size("dp")
    parts = lax.axis_size("seq")
    half = parts // 2
    group = lax.axis_index("dp")
    position = lax.axis_index("seq")

    def place(base, clip, quarter):
        return (2 * base + quarter % 2) * parts + clip * half + quarter // 2

    def home(base, clip, quarter):
        return (2 * base + clip) * parts + quarter

    spots = [
        (base, clip, quarter)
        for base in range(groups // 2)
        for clip in range(2)
        for quarter in range(parts)
    ]
    leave = [(home(*spot), place(*spot)) for spot in spots]
    back = [(target, source) for source, target in leave]

    def partner(values, step):
        pairs = [
            (place(base, clip, quarter), place(base, clip, quarter ^ step))
            for base, clip, quarter in spots
        ]
        return lax.ppermute(values, BOTH, pairs)

    def spread(values):
        if parts != 4:
            return [values] + [partner(values, step) for step in range(1, parts)]
        across_chips = partner(values, 2)
        return [values, partner(values, 1), across_chips, partner(across_chips, 1)]

    columns = []
    for layer in range(layers):
        for member in (
            norm1_gain,
            norm1_shift,
            query_bias,
            value_bias,
            out_bias,
            norm2_gain,
            norm2_shift,
            proj_bias,
        ):
            columns.append(member[layer].reshape(rows, 1))
        columns.append(hidden_bias[layer].reshape(rows, ways))
    used = layers * (VECTORS + ways)
    columns.append(jnp.zeros((rows, SMALL - used), BF16))
    sum_rows = -(-used // 8) * 8
    attn_packed, mlp_packed = [], []
    for layer in range(layers):
        members = [
            query_weight[layer],
            key_weight[layer],
            value_weight[layer],
        ]
        if layer == 0:
            members += columns
        attn_packed.append(jnp.concatenate(members, axis=1))
        mlp_packed.append(
            jnp.concatenate(
                [
                    out_weight[layer],
                    deinterleave(hidden_weight[layer], ways),
                    proj_weight[layer].reshape(rows, ways * width),
                ],
                axis=1,
            )
        )
    small_at = 3 * width

    block = parts * rows
    direct = groups == 8 and parts == 4 and layers == 2 and block % 32 == 0 and rows % 8 == 0
    own_bits = jnp.stack([(group >> bit) & 1 for bit in range(3)]).astype(jnp.int32)

    def exchange(values, flip):
        pairs = [(device, device ^ flip) for device in range(groups * parts)]
        return lax.ppermute(values, BOTH, pairs)

    core, across, along = parts, 2 * parts, 4 * parts

    class Gather:
        def __init__(self, base, column, columns):
            self.base = base
            self.place = (column, columns)

        def start(self, whole=False):
            self.near = [self.base, exchange(self.base, across), exchange(self.base, along)]
            if whole:
                self.near.append(exchange(self.base, across + along))

        def finish(self, ahead=()):
            upper, lower, joined = relay(*self.near, ahead)
            self.sends = [upper, lower]
            self.near += [exchange(upper, across), exchange(lower, along)]
            self.far = [exchange(joined, core)]

        def close(self, ahead=()):
            self.far.append(exchange(join(self.near[3:], ahead), core))

        def gather(self, ahead=()):
            self.joined = [join(self.near[:2], ahead), join(self.near[2:], ahead)]

        def source(self):
            plan = [(index, None, 2 * index, 0, block) for index in range(3)]
            if len(self.near) == 4:
                far = [exchange(member, core) for member in self.joined]
                plan.append((3, None, 6, 0, block))
                plan += [
                    (4 + index // 2, index % 2, 2 * index + 1, 0, block) for index in range(4)
                ]
                return Source(self.near + far, plan, block)
            half = block // 2
            plan += [(3 + index, None, 6, index * half, half) for index in range(2)]
            plan += [(5, index, 2 * index + 1, 0, block) for index in range(3)]
            plan += [(6, index, 7, index * half, half) for index in range(2)]
            return Source(self.near + self.far, plan, block)

    def gather_layer(layer):
        shard = jnp.concatenate([attn_packed[layer], mlp_packed[layer]], axis=1)
        return lax.all_gather(shard, BOTH, axis=0, tiled=True)

    queue = []
    if direct:
        shards = [shard for pair in zip(attn_packed, mlp_packed) for shard in pair]
        sizes = [shard.shape[1] for shard in shards]
        members = [shards[0]] + [exchange(shards[0], step) for step in range(1, parts)]
        queue = [Gather(assemble(members, ()), 0, sizes[0])]
        rows_two = lax.all_gather(shards[1], "seq", axis=0, tiled=True)
        queue.append(Gather(rows_two, 0, sizes[1]))
        queue[0].start(True)
        queue[0].gather()
        later = hold(jnp.concatenate(shards[2:], axis=1), 0, sum(sizes[2:]), [queue[0].base])
        later = lax.all_gather(later, "seq", axis=0, tiled=True)
        queue += [Gather(later, 0, sizes[2]), Gather(later, sizes[2], sizes[3])]
    else:
        gathered = [gather_layer(layer) for layer in range(layers)]
    raw = lax.ppermute(inputs.reshape(frames, width), BOTH, leave)
    raw_blocks = spread(raw)

    def follow(part, ahead, whole=False):
        part.base = long(hold, part.base, *part.place, ahead)
        part.start(whole)
        return [part.base]

    own, blocks, saved, small = raw, raw_blocks, [], None
    for layer in range(layers):
        last = layer == layers - 1
        mlp_at = attn_packed[layer].shape[1]
        source = queue[2 * layer].source() if direct else Source([gathered[layer]])
        ahead = []
        if direct:
            present = queue[2 * layer + 1]
            ahead = follow(present, []) if layer == 0 else [present.base]
        q, k, v, a1_full, small, w_qkv = (long if layer == 0 else plain)(
            forward_qkv, layer, layers, ways, blocks, small, source, small_at, ahead
        )
        ahead = []
        if direct and layer > 0:
            present.finish([q])
            ahead = present.sends
        lse, o = (plain if layer == 0 else long)(forward_heads, q, k, v, ahead)
        ahead = []
        if direct:
            if layer == 0:
                present.finish([lse])
            present.close([lse])
            source, mlp_at = present.source(), 0
            if not last:
                ahead = follow(queue[2 * layer + 2], present.near[3:], True)
                ahead += follow(queue[2 * layer + 3], ahead)
        h1, a2, g, slope, following, a1_next, w_mlp, mlp_at = long(
            forward_mlp, layer, last, ways, own, o, small, source, mlp_at, ahead
        )
        w_out, out_at, mlp_at = w_mlp, mlp_at, mlp_at + width
        coming = [] if last else spread(a1_next)
        if direct and not last:
            queue[2 * layer + 2].gather([a1_next])
        if layer == 0:
            top = hold(cotangent.reshape(frames, width), 0, width, [a2])
            top = lax.ppermute(top, BOTH, leave)
        saved.append(
            (
                own,
                a1_full,
                q,
                k,
                v,
                lse,
                o,
                h1,
                a2,
                g,
                slope,
                w_qkv,
                w_out,
                out_at,
                w_mlp,
                mlp_at,
            )
        )
        own = following
        blocks = coming
    final = lax.ppermute(own, BOTH, back)

    class Chain:
        def __init__(self, terms, beside=False):
            self.beside = beside
            self.stage = 0 if len(terms) == 2 else 4
            self.total = None
            if len(terms) == 2:
                self.kept = [terms[0]]
                self.received = [exchange(terms[1], core)]
            else:
                self.total = lax.psum_scatter(
                    terms[0], BOTH, scatter_dimension=0, tiled=True
                ).astype(F32)

        def step(self, ahead=()):
            self.stage += 1
            if self.stage < 3:
                left, left_send, right, right_send = add_halves(
                    own_bits, self.kept, self.received, self.stage, ahead
                )
                turns = (across, along) if self.stage == 1 else (along, across)
                self.kept = [left, right]
                self.received = [exchange(left_send, turns[0]), exchange(right_send, turns[1])]
                return [left_send, right_send]
            if self.stage == 3 and self.beside:
                block_terms = add_block(self.kept, self.received, ahead)
                self.kept, self.received = [
                    lax.psum_scatter(block_terms, "seq", scatter_dimension=0, tiled=True)
                ], []
                self.stage = 4
                return [block_terms]
            if self.stage == 3:
                mine, send = add_rows(self.kept, self.received, parts, ahead)
                self.kept, self.received = [mine], [exchange(send, 1)]
            else:
                mine, send = add_ends(self.kept[0], self.received[0], ahead)
                self.kept, self.received = [mine], [exchange(send, 2)]
            return [send]

        def members(self):
            return self.kept + self.received if self.total is None else [self.total]

    split = block if direct else 0
    sums = jnp.zeros((sum_rows, width), F32)
    above = [top]
    mlp_chains, attn_chains = [None] * layers, [None] * layers
    done = []

    def steps(*chains):
        nonlocal done
        for chain in chains:
            if chain is not None and chain.stage < 4:
                done = [*chain.step(done), *done[:1]]

    def close(chain):
        nonlocal done
        if chain is not None and chain.total is None:
            while chain.stage < 4:
                steps(chain)
            chain.total = add_parts(chain.kept + chain.received, done)
            done = [chain.total]

    middle = HEADS // 4
    for layer in reversed(range(layers)):
        (
            own,
            a1_full,
            q,
            k,
            v,
            lse,
            o,
            h1,
            a2,
            g,
            slope,
            w_qkv,
            w_out,
            out_at,
            w_mlp,
            mlp_at,
        ) = saved[layer]
        upper_attn = None if layer == layers - 1 else attn_chains[layer + 1]
        upper_mlp = None if layer == layers - 1 else mlp_chains[layer + 1]
        terms, dh1, sums = long(
            backward_mlp,
            layer,
            ways,
            above,
            small,
            sums,
            h1,
            a2,
            g,
            slope,
            w_mlp,
            mlp_at,
            split,
            done,
        )
        mlp_chains[layer] = Chain(terms, layer > 0)
        done = list(terms[-1:])
        if layer == layers - 1:
            done.append(final)
        steps(upper_attn)
        before = []
        given, dz = dh1, None
        for pairs in ((0, middle), (middle, PAIRS)):
            part, sums, opened, da = long(
                backward_attention,
                layer,
                ways,
                given,
                q,
                k,
                v,
                lse,
                raw_blocks if layer == 0 else [],
                small,
                sums,
                w_qkv,
                w_out,
                out_at,
                pairs,
                before,
                done,
            )
            before = before + [part]
            if opened:
                dz, given = opened
            done = [sums]
            if not da:
                steps(mlp_chains[layer], upper_attn, upper_mlp)
        siblings = partner(da[1], 1)

        def cross():
            nonlocal done
            crossing = add_cross(da[2], siblings, done)
            done = [crossing]
            return partner(crossing, 2)

        if layer > 0:
            crossed = cross()
        else:
            steps(mlp_chains[layer], upper_attn)
            close(upper_mlp)
        terms = attention_grads(
            a1_full,
            o,
            dz,
            before,
            sums if layer == 0 else None,
            split,
            done,
        )
        attn_chains[layer] = Chain(terms)
        done = list(terms[-1:])
        if layer > 0:
            steps(mlp_chains[layer])
        else:
            steps(upper_attn)
            long(steps, mlp_chains[layer])
            crossed = cross()
            steps(attn_chains[layer])
        above = [dh1, da[0], own, siblings, crossed]
    grad_rows = long(finish_rows, raw, above[0], small, [above[1], *above[3:]], done)
    done = [grad_rows]
    grad_rows = lax.ppermute(grad_rows, BOTH, back).astype(F32)
    steps(attn_chains[0], mlp_chains[0], attn_chains[0])
    for chain in attn_chains[1:]:
        close(chain)
    steps(attn_chains[0])
    for chain in attn_chains + mlp_chains:
        while chain.stage < 4:
            steps(chain)
    table = spread_matrix(ways)
    grad_hidden, grad_proj = finish_mlp(
        [chain.members() for chain in mlp_chains], table, ways, done
    )
    weights, vectors, biases = finish_attention(
        [chain.members() for chain in attn_chains], ways, [grad_hidden]
    )
    grad_hbias = biases.transpose(0, 2, 1).reshape(layers, rows * ways)
    return (
        final.reshape(inputs.shape),
        grad_rows.reshape(inputs.shape),
        vectors[0],
        vectors[1],
        weights[0],
        vectors[2],
        weights[1],
        weights[2],
        vectors[3],
        weights[3],
        vectors[4],
        vectors[5],
        vectors[6],
        grad_hidden,
        grad_hbias,
        grad_proj,
        vectors[7],
    )


def solution(mesh):
    rows = P("dp", "seq", None)
    vector = P(None, BOTH)
    matrix = P(None, BOTH, None)
    params = (
        vector,
        vector,
        matrix,
        vector,
        matrix,
        matrix,
        vector,
        matrix,
        vector,
        vector,
        vector,
        matrix,
        vector,
        matrix,
        vector,
    )
    return jax.shard_map(
        body,
        mesh=mesh,
        in_specs=(rows, rows) + params,
        out_specs=(rows, rows) + params,
        check_vma=False,
    )
```

time: 2650 us -> 493 us (0.19)
  waiting for transfers between devices: 2280 us -> 91.2 us
  Pallas kernels: 0 us -> 267 us
  matrix products: 188 us -> 0.47 us
  starting transfers between devices: 2.2 us -> 81.7 us
  other arithmetic: 55.7 us -> 2.27 us
  blocking collectives: 43.4 us -> 0 us
  local copies, waits for them, and re-layouts: 58.4 us -> 28.8 us
    reduce_scatter x16 -> x1, waiting for transfers between devices: 1400 us -> 0.01 us  [step(): lax.psum_scatter(block_terms, 'seq', scatter_dimension=0, tiled=True)]
    all_gather x16 -> x2, waiting for transfers between devices: 716 us -> 0.01 us  [the longest x1 0.01 us: body(): rows_two = lax.all_gather(shards[1], 'seq', axis=0, tiled=True)]
    pallas_call x0 -> x50, Pallas kernels: none -> 267 us  [the longest x42 228 us: call(): pl.pallas_call(used, name=name, cost_estimate=cost(), out_shape=outs, in_...]
    dot_general x48 -> x2, matrix products: 188 us -> 0.47 us  [mm(): lax.dot_general(left_side, right_side, (((1,), (0,)), ((), ())), preferre...]
    unnamed x34 -> x3, waiting for transfers between devices: 156 us -> 0.05 us
    ppermute x0 -> x65, waiting for transfers between devices: none -> 91.2 us  [the longest x51 73.2 us: exchange(): return lax.ppermute(values, BOTH, pairs)]
    ppermute x0 -> x65, starting transfers between devices: none -> 81.5 us  [the longest x51 48 us: exchange(): return lax.ppermute(values, BOTH, pairs)]
    unnamed x1 -> x0, blocking collectives: 43.4 us -> none
  transfers between devices with their start and end apart: 33 -> 68, of which waited for: 31 -> 20; matrix products, arithmetic and copies ran while one was open for 8% -> 1% of each run, Pallas kernels for 0% -> 52%
where the time goes in v1:
time: 493 us; the launch traced here: 486 us
  Pallas kernels  267 us (54%)
  waiting for transfers between devices  91.2 us (18%)
  starting transfers between devices  81.7 us (17%)
  local copies, waits for them, and re-layouts  28.8 us (6%)
  between operations  14.8 us (3%)
    pallas_call x42, Pallas kernels, call(): pl.pallas_call(used, name=name, cost_estimate=cost(), out_shape=outs, in_...  228 us
    ppermute x51, waiting for transfers between devices, exchange(): return lax.ppermute(values, BOTH, pairs)  73.2 us
    ppermute x51, starting transfers between devices, exchange(): return lax.ppermute(values, BOTH, pairs)  48 us
    pallas_call x8, Pallas kernels, add_halves(): pl.pallas_call(kernel, name='add_halves', cost_estimate=cost(), out_shape...  38.5 us
    ppermute x10, starting transfers between devices, partner(): return lax.ppermute(values, BOTH, pairs)  24.6 us
    unnamed x118, local copies, waits for them, and re-layouts  21.6 us
    ppermute x10, waiting for transfers between devices, partner(): return lax.ppermute(values, BOTH, pairs)  18 us
  transfers between devices with their start and end apart: 68, of which 20 were waited for; matrix products, arithmetic and copies ran while one was open for 1% of the time, Pallas kernels for 52%

profile of v1, /device:TPU:0, one launch (start us, length us, event | category | flops | bytes accessed | tf_op | source)
XLA Modules:
  0.0 485.8 jit_solution(14728568802327937842)
XLA Ops:
  18.9 4.5 collective-permute-start
  24.2 11.4 %collective-permute-done.5.refs_2_ = bf16[24,2432]{1,0:T(8,128)(2,1)S(1)} collective-permute-done((bf16[24,2432]{1,0:T(8,128)(2,1)S(1)}, bf16[24,2432]{1,0:T(8,128)(2,1)S(1)}, u32[]{:S(2)}, u32[]{:S(2)}) %collective-permute-start.5) | collective-permute-done | bytes 116768 | tf_op jit(solution)/shard_map/ppermute | solution.py:1121
  42.3 17.6 %collective-permute-start.2 = (bf16[256,768]{1,0:T(8,128)(2,1)}, bf16[256,768]{1,0:T(8,128)(2,1)}, u32[]{:S(2)}, u32[]{:S(2)}) collective-permute-start(bf16[256,768]{1,0:T(8,128)(2,1)} %collective-permute-done.refs_0_.refs_9_), channel_id=1, source_target_pairs={{0,1},{4,5},{1,0},{5,4},{2,3},{6,7},{3,2},{7,6},{8,9},{12,13},{9,8... | collective-permute-start | bytes 1179656 | tf_op jit(solution)/shard_map/ppermute | solution.py:1068
  76.0 8.8 %forward_qkv.2 = (bf16[256,768]{1,0:T(8,128)(2,1)}, bf16[1024,768]{1,0:T(8,128)(2,1)}, bf16[1024,768]{1,0:T(8,128)(2,1)}, bf16[1024,768]{1,0:T(8,128)(2,1)}, f32...) custom-call(bf16[256,768]{1,0:T(8,128)(2,1)} %collective-permute-done.refs_0_.refs_9_, ...), custom_call_target="tpu_custom_call" | custom-call | flops 109999996928 | bytes 300000000 | tf_op jit(solution)/shard_map/forward_qkv/pallas_call | solution.py:121
  84.8 11.8 %forward_heads.2 = (f32[8,512]{1,0:T(8,128)}, bf16[256,768]{1,0:T(8,128)(2,1)}) custom-call(bf16[256,768]{1,0:T(8,128)(2,1)} %get-tuple-element.148.refs_0_.refs_1_, bf16[1024,768]{1,0:T(8,128)(2,1)} %get-tuple-element.149.refs_1_.refs_2_, bf16[1024,768]{1,0:T(8,128)(2,1)} %get-tuple-element.150.refs_2_.refs_3_), custom_call_target="tpu_custom_call" | custom-call | flops 55000000 | bytes 150000 | tf_op jit(solution)/shard_map/forward_heads/pallas_call | solution.py:121
  96.7 6.8 %collective-permute-done.12.refs_1_.refs_4_ = bf16[96,6912]{1,0:T(8,128)(2,1)S(1)} collective-permute-done((bf16[96,6912]{1,0:T(8,128)(2,1)}, bf16[96,6912]{1,0:T(8,128)(2,1)S(1)}, u32[]{:S(2)}, u32[]{:S(2)}) %collective-permute-start.12) | collective-permute-done | bytes 1327136 | tf_op jit(solution)/shard_map/ppermute | solution.py:1121
  104.8 4.6 relay.2
  112.3 13.3 %collective-permute-done.14.refs_0_.refs_1_.refs_6_ = bf16[48,6912]{1,0:T(8,128)(2,1)S(1)} collective-permute-done((bf16[48,6912]{1,0:T(8,128)(2,1)}, bf16[48,6912]{1,0:T(8,128)(2,1)S(1)}, u32[]{:S(2)}, u32[]{:S(2)}) %collective-permute-start.14) | collective-permute-done | bytes 663584 | tf_op jit(solution)/shard_map/ppermute | solution.py:1121
  141.9 11.7 %forward_mlp.2 = (f32[256,768]{1,0:T(8,128)}, bf16[256,768]{1,0:T(8,128)(2,1)}, bf16[256,3072]{1,0:T(8,128)(2,1)}, bf16[256,3072]{1,0:T(8,128)(2,1)}, f32[256,76...) custom-call(bf16[256,768]{1,0:T(8,128)(2,1)} %collective-permute-done.refs_0_.refs_9_, ...), custom_call_target="tpu_custom_call" | custom-call | flops 109999996928 | bytes 300000000 | tf_op jit(solution)/shard_map/forward_mlp/pallas_call | solution.py:121
  160.4 9.7 %collective-permute-done.19.refs_2_ = bf16[256,768]{1,0:T(8,128)(2,1)S(1)} collective-permute-done((bf16[256,768]{1,0:T(8,128)(2,1)S(1)}, bf16[256,768]{1,0:T(8,128)(2,1)S(1)}, u32[]{:S(2)}, u32[]{:S(2)}) %collective-permute-start.19) | collective-permute-done | bytes 393248 | tf_op jit(solution)/shard_map/ppermute | solution.py:1068
  173.3 8.7 %forward_qkv.3 = (bf16[256,768]{1,0:T(8,128)(2,1)}, bf16[1024,768]{1,0:T(8,128)(2,1)}, bf16[1024,768]{1,0:T(8,128)(2,1)}, bf16[1024,768]{1,0:T(8,128)(2,1)}, bf16[768,2304]{1,0:T(8,128)(2,1)}) custom-call(bf16[256,768]{1,0:T(8,128)(2,1)} %get-tuple-element.158.refs_2_.refs_0_, bf16[256,768]{1,0:T(8,128)(2,1)} %collective-permute-done.18.refs_1_, ...), custom_call_target="tpu_custom_call" | custom-call | flops 55000000 | bytes 150000 | tf_op jit(solution)/shard_map/forward_qkv/pallas_call | solution.py:121
  183.2 4.4 relay.3
  189.0 11.5 %forward_heads.3 = (f32[8,512]{1,0:T(8,128)}, bf16[256,768]{1,0:T(8,128)(2,1)}) custom-call(bf16[256,768]{1,0:T(8,128)(2,1)} %get-tuple-element.159.refs_3_.refs_0_.refs_1_, bf16[1024,768]{1,0:T(8,128)(2,1)} %get-tuple-element.160.refs_1_.refs_2_, bf16[1024,768]{1,0:T(8,128)(2,1)} %get-tuple-element.161.refs_2_.refs_3_, ...), custom_call_target="tpu_custom_call" | custom-call | flops 109999996928 | bytes 300000000 | tf_op jit(solution)/shard_map/forward_heads/pallas_call | solution.py:121
  214.3 11.7 %forward_mlp.3 = (f32[256,768]{1,0:T(8,128)}, bf16[256,768]{1,0:T(8,128)(2,1)}, bf16[256,3072]{1,0:T(8,128)(2,1)}, bf16[256,3072]{1,0:T(8,128)(2,1)}, bf16[256,7...) custom-call(f32[256,768]{1,0:T(8,128)} %get-tuple-element.157.refs_0_.refs_2_, bf16[256,768]{1,0:T(8,128)(2,1)} %get-tuple-element.164.refs_1_, ...), custom_call_target="tpu_custom_call" | custom-call | flops 109999996928 | bytes 300000000 | tf_op jit(solution)/shard_map/forward_mlp/pallas_call | solution.py:121
  228.5 14.5 %backward_mlp.2 = (bf16[4,96,6144]{2,1,0:T(8,128)(2,1)}, bf16[4,96,6144]{2,1,0:T(8,128)(2,1)}, f32[256,768]{1,0:T(8,128)}, f32[24,768]{1,0:T(8,128)}) custom-call(bf16[256,768]{1,0:T(8,128)(2,1)} %copy-done.54, f32[24,768]{1,0:T(8,128)} %get-tuple-element.152.refs_2_.refs_4_.refs_1_.refs_5_, f32[24,768]{1,0:T(8,128)} %broadcast_in_dim.7.refs_2_, ...), custom_call_target="tpu_custom_call" | custom-call | flops 109999996928 | bytes 300000000 | tf_op jit(solution)/shard_map/backward_mlp/pallas_call | solution.py:121
  246.6 10.8 %backward_attention.4 = (bf16[256,384]{1,0:T(8,128)(2,1)}, bf16[1024,384]{1,0:T(8,128)(2,1)}, bf16[1024,384]{1,0:T(8,128)(2,1)}, f32[24,768]{1,0:T(8,128)}, bf16...) custom-call(f32[256,768]{1,0:T(8,128)} %get-tuple-element.174.refs_0_, ...), custom_call_target="tpu_custom_call" | custom-call | flops 109999996928 | bytes 300000000 | tf_op jit(solution)/shard_map/backward_attention/pallas_call | solution.py:121
  257.5 7.0 %add_halves.8 = (bf16[2,96,3072]{2,1,0:T(8,128)(2,1)}, bf16[2,96,3072]{2,1,0:T(8,128)(2,1)}, bf16[2,96,3072]{2,1,0:T(8,128)(2,1)}, bf16[2,96,3072]{2,1,0:T(8,128)(2,1)}) custom-call(s32[3]{0:T(128)} %pad_add_fusion.own, bf16[4,96,6144]{2,1,0:T(8,128)(2,1)} %get-tuple-element.183.refs_0_.refs_2_.refs_4_.refs_6_, ...), custom_call_target="tpu_custom_call" | custom-call | flops 55000000 | bytes 150000 | tf_op jit(solution)/shard_map/add_halves/pallas_call | solution.py:836
  266.2 12.9 %backward_attention.5 = (bf16[256,384]{1,0:T(8,128)(2,1)}, bf16[1024,384]{1,0:T(8,128)(2,1)}, bf16[1024,384]{1,0:T(8,128)(2,1)}, f32[24,768]{1,0:T(8,128)}, f32[...) custom-call(bf16[256,768]{1,0:T(8,128)(2,1)} %get-tuple-element.177.refs_0_, ...), custom_call_target="tpu_custom_call" | custom-call | flops 109999996928 | bytes 300000000 | tf_op jit(solution)/shard_map/backward_attention/pallas_call | solution.py:121
  287.2 8.2 %attention_grads.2 = (bf16[4,96,3072]{2,1,0:T(8,128)(2,1)}, bf16[4,96,3072]{2,1,0:T(8,128)(2,1)}) custom-call(bf16[1024,768]{1,0:T(8,128)(2,1)} %get-tuple-element.196.refs_0_, bf16[256,768]{1,0:T(8,128)(2,1)} %get-tuple-element.164.refs_1_, bf16[256,768]{1,0:T(8,128)(2,1)} %get-tuple-element.197.refs_2_, ...), custom_call_target="tpu_custom_call" | custom-call | flops 55000000 | bytes 150000 | tf_op jit(solution)/shard_map/attention_grads/pallas_call | solution.py:121
  296.6 4.4 add_halves.9
  304.3 15.5 %backward_mlp.3 = (bf16[4,96,6144]{2,1,0:T(8,128)(2,1)}, bf16[4,96,6144]{2,1,0:T(8,128)(2,1)}, f32[256,768]{1,0:T(8,128)}, f32[24,768]{1,0:T(8,128)}) custom-call(f32[256,768]{1,0:T(8,128)} %get-tuple-element.174.refs_0_, f32[256,768]{1,0:T(8,128)} %get-tuple-element.186.refs_1_, f32[256,768]{1,0:T(8,128)} %get-tuple-element.157.refs_0_.refs_2_, ...), custom_call_target="tpu_custom_call" | custom-call | flops 109999996928 | bytes 300000000 | tf_op jit(solution)/shard_map/backward_mlp/pallas_call | solution.py:121
  319.9 4.3 add_halves.10
  325.9 10.6 %backward_attention.6 = (bf16[256,384]{1,0:T(8,128)(2,1)}, bf16[1024,384]{1,0:T(8,128)(2,1)}, bf16[1024,384]{1,0:T(8,128)(2,1)}, f32[24,768]{1,0:T(8,128)}, bf16...) custom-call(f32[256,768]{1,0:T(8,128)} %get-tuple-element.204.refs_0_.refs_1_, ...), custom_call_target="tpu_custom_call" | custom-call | flops 109999996928 | bytes 300000000 | tf_op jit(solution)/shard_map/backward_attention/pallas_call | solution.py:121
  336.5 7.0 %add_halves.11 = (bf16[2,96,3072]{2,1,0:T(8,128)(2,1)}, bf16[2,96,3072]{2,1,0:T(8,128)(2,1)}, bf16[2,96,3072]{2,1,0:T(8,128)(2,1)}, bf16[2,96,3072]{2,1,0:T(8,128)(2,1)}) custom-call(s32[3]{0:T(128)} %pad_add_fusion.own, bf16[4,96,6144]{2,1,0:T(8,128)(2,1)} %get-tuple-element.220.refs_0_.refs_2_.refs_4_.refs_6_, ...), custom_call_target="tpu_custom_call" | custom-call | flops 55000000 | bytes 150000 | tf_op jit(solution)/shard_map/add_halves/pallas_call | solution.py:836
  354.3 13.9 %backward_attention.7 = (bf16[256,384]{1,0:T(8,128)(2,1)}, bf16[1024,384]{1,0:T(8,128)(2,1)}, bf16[1024,384]{1,0:T(8,128)(2,1)}, f32[24,768]{1,0:T(8,128)}, f32[...) custom-call(bf16[256,768]{1,0:T(8,128)(2,1)} %get-tuple-element.210.refs_0_, ...), custom_call_target="tpu_custom_call" | custom-call | flops 109999996928 | bytes 300000000 | tf_op jit(solution)/shard_map/backward_attention/pallas_call | solution.py:121
  368.2 4.5 collective-permute-done.46.refs_1_.refs_3_
  373.7 4.3 add_halves.13
  385.8 8.2 %attention_grads.3 = (bf16[4,96,3328]{2,1,0:T(8,128)(2,1)}, bf16[4,96,3328]{2,1,0:T(8,128)(2,1)}) custom-call(bf16[1024,768]{1,0:T(8,128)(2,1)} %get-tuple-element.239.refs_0_, bf16[256,768]{1,0:T(8,128)(2,1)} %get-tuple-element.151.refs_1_, bf16[256,768]{1,0:T(8,128)(2,1)} %get-tuple-element.240.refs_2_, ...), custom_call_target="tpu_custom_call" | custom-call | flops 55000000 | bytes 150000 | tf_op jit(solution)/shard_map/attention_grads/pallas_call | solution.py:121
  405.2 4.6 add_halves.14
  419.2 6.7 %collective-permute-done.56.refs_1_.refs_3_ = bf16[2,96,1664]{2,1,0:T(8,128)(2,1)S(1)} collective-permute-done((bf16[2,96,1664]{2,1,0:T(8,128)(2,1)}, bf16[2,96,1664]{2,1,0:T(8,128)(2,1)S(1)}, u32[]{:S(2)}, u32[]{:S(2)}) %collective-permute-start.56) | collective-permute-done | bytes 639008 | tf_op jit(solution)/shard_map/ppermute | solution.py:1121
  447.0 13.0 %collective-permute-done.62.refs_1_ = bf16[24,3072]{1,0:T(8,128)(2,1)S(1)} collective-permute-done((bf16[24,3072]{1,0:T(8,128)(2,1)S(1)}, bf16[24,3072]{1,0:T(8,128)(2,1)S(1)}, u32[]{:S(2)}, u32[]{:S(2)}) %collective-permute-start.62) | collective-permute-done | bytes 147488 | tf_op jit(solution)/shard_map/ppermute | solution.py:1121
  470.1 4.2 finish_mlp.1
  (328 shorter events, 179.6 us)
Async XLA Ops:
  7.2 62.5 %all-gather.3.cloned.1.call-start = ((), (), s32[]{:S(2)}) async-start(), calls=%async_computation.1 | async-start | bytes 1658880 | tf_op jit(solution)/shard_map/all_gather | solution.py:1172
  11.1 101.2 %all-gather.5.cloned.1.call-start = ((), (), s32[]{:S(2)}) async-start(), calls=%async_computation.2 | async-start | bytes 2211840 | tf_op jit(solution)/shard_map/all_gather | solution.py:1177
  18.9 23.3 %collective-permute-start = (bf16[256,768]{1,0:T(8,128)(2,1)}, bf16[256,768]{1,0:T(8,128)(2,1)}, u32[]{:S(2)}, u32[]{:S(2)}) collective-permute-start(bf16[256,768]{1,0:T(8,128)(2,1)} %bitcast), channel_id=1, source_target_pairs={{0,0},{1,4},{2,1},{3,5},{4,2},{5,6},{6,3},{7,7},{8,8},{9,12},{10,9... | collective-permute-start | bytes 1179656 | tf_op jit(solution)/shard_map/ppermute | solution.py:1181
  38.8 24.0 %collective-permute-start.7 = (bf16[96,2432]{1,0:T(8,128)(2,1)}, bf16[96,2432]{1,0:T(8,128)(2,1)S(1)}, u32[]{:S(2)}, u32[]{:S(2)}) collective-permute-start(bf16[96,2432]{1,0:T(8,128)(2,1)} %bitcast.73), channel_id=1, source_target_pairs={{0,8},{1,9},{2,10},{3,11},{4,12},{5,13},{6,14},{7,15},{8,0},{9,1},... | collective-permute-start | bytes 1400840 | tf_op jit(solution)/shard_map/ppermute | solution.py:1121
  40.3 26.0 %collective-permute-start.8 = (bf16[96,2432]{1,0:T(8,128)(2,1)}, bf16[96,2432]{1,0:T(8,128)(2,1)S(1)}, u32[]{:S(2)}, u32[]{:S(2)}) collective-permute-start(bf16[96,2432]{1,0:T(8,128)(2,1)} %bitcast.74), channel_id=1, source_target_pairs={{0,16},{1,17},{2,18},{3,19},{4,20},{5,21},{6,22},{7,23},{8,24},{9,... | collective-permute-start | bytes 1400840 | tf_op jit(solution)/shard_map/ppermute | solution.py:1121
  41.7 24.5 %collective-permute-start.9 = (bf16[96,2432]{1,0:T(8,128)(2,1)}, bf16[96,2432]{1,0:T(8,128)(2,1)}, u32[]{:S(2)}, u32[]{:S(2)}) collective-permute-start(bf16[96,2432]{1,0:T(8,128)(2,1)} %bitcast.75), channel_id=1, source_target_pairs={{0,24},{1,25},{2,26},{3,27},{4,28},{5,29},{6,30},{7,31},{8,16},{9,... | collective-permute-start | bytes 1400840 | tf_op jit(solution)/shard_map/ppermute | solution.py:1121
  42.3 26.9 %collective-permute-start.2 = (bf16[256,768]{1,0:T(8,128)(2,1)}, bf16[256,768]{1,0:T(8,128)(2,1)}, u32[]{:S(2)}, u32[]{:S(2)}) collective-permute-start(bf16[256,768]{1,0:T(8,128)(2,1)} %collective-permute-done.refs_0_.refs_9_), channel_id=1, source_target_pairs={{0,1},{4,5},{1,0},{5,4},{2,3},{6,7},{3,2},{7,6},{8,9},{12,13},{9,8... | collective-permute-start | bytes 1179656 | tf_op jit(solution)/shard_map/ppermute | solution.py:1068
  62.6 321.3 %reduce-scatter.2.cloned.1.call-start = ((), (), s32[]{:S(2)}) async-start(), calls=%async_computation.3 | async-start | bytes 1474560 | tf_op jit(solution)/shard_map/reduce_scatter | solution.py:1275
  72.2 31.3 %collective-permute-start.12 = (bf16[96,6912]{1,0:T(8,128)(2,1)}, bf16[96,6912]{1,0:T(8,128)(2,1)S(1)}, u32[]{:S(2)}, u32[]{:S(2)}) collective-permute-start(bf16[96,6912]{1,0:T(8,128)(2,1)} %hold.5.refs_10_.refs_0_.refs_3_), channel_id=1, source_target_pairs={{0,8},{1,9},{2,10},{3,11},{4,12},{5,13},{6,14},{7,15},{8,0},{9,1},... | collective-permute-start | bytes 3981320 | tf_op jit(solution)/shard_map/ppermute | solution.py:1121
  73.7 31.1 %collective-permute-start.13 = (bf16[96,6912]{1,0:T(8,128)(2,1)}, bf16[96,6912]{1,0:T(8,128)(2,1)}, u32[]{:S(2)}, u32[]{:S(2)}) collective-permute-start(bf16[96,6912]{1,0:T(8,128)(2,1)} %hold.5.refs_10_.refs_0_.refs_3_), channel_id=1, source_target_pairs={{0,16},{1,17},{2,18},{3,19},{4,20},{5,21},{6,22},{7,23},{8,24},{9,... | collective-permute-start | bytes 3981320 | tf_op jit(solution)/shard_map/ppermute | solution.py:1121
  112.2 28.1 %collective-permute-start.16 = (bf16[3,96,6912]{2,1,0:T(8,128)(2,1)}, bf16[3,96,6912]{2,1,0:T(8,128)(2,1)}, u32[]{:S(2)}, u32[]{:S(2)}) collective-permute-start(bf16[3,96,6912]{2,1,0:T(8,128)(2,1)} %get-tuple-element.156), channel_id=1, source_target_pairs={{0,4},{1,5},{2,6},{3,7},{4,0},{5,1},{6,2},{7,3},{8,12},{9,13},{10,... | collective-permute-start | bytes 11943944 | tf_op jit(solution)/shard_map/ppermute | solution.py:1121
  129.9 23.7 %collective-permute-start.21 = (bf16[96,2304]{1,0:T(8,128)(2,1)}, bf16[96,2304]{1,0:T(8,128)(2,1)}, u32[]{:S(2)}, u32[]{:S(2)}) collective-permute-start(bf16[96,2304]{1,0:T(8,128)(2,1)} %hold.7.refs_1_.refs_10_.refs_0_.refs_5_), channel_id=1, source_target_pairs={{0,8},{1,9},{2,10},{3,11},{4,12},{5,13},{6,14},{7,15},{8,0},{9,1},... | collective-permute-start | bytes 1327112 | tf_op jit(solution)/shard_map/ppermute | solution.py:1121
  131.0 24.9 %collective-permute-start.22 = (bf16[96,2304]{1,0:T(8,128)(2,1)}, bf16[96,2304]{1,0:T(8,128)(2,1)}, u32[]{:S(2)}, u32[]{:S(2)}) collective-permute-start(bf16[96,2304]{1,0:T(8,128)(2,1)} %hold.7.refs_1_.refs_10_.refs_0_.refs_5_), channel_id=1, source_target_pairs={{0,16},{1,17},{2,18},{3,19},{4,20},{5,21},{6,22},{7,23},{8,24},{9,... | collective-permute-start | bytes 1327112 | tf_op jit(solution)/shard_map/ppermute | solution.py:1121
  132.5 23.9 %collective-permute-start.23 = (bf16[96,2304]{1,0:T(8,128)(2,1)}, bf16[96,2304]{1,0:T(8,128)(2,1)}, u32[]{:S(2)}, u32[]{:S(2)}) collective-permute-start(bf16[96,2304]{1,0:T(8,128)(2,1)} %hold.7.refs_1_.refs_10_.refs_0_.refs_5_), channel_id=1, source_target_pairs={{0,24},{1,25},{2,26},{3,27},{4,28},{5,29},{6,30},{7,31},{8,16},{9,... | collective-permute-start | bytes 1327112 | tf_op jit(solution)/shard_map/ppermute | solution.py:1121
  139.3 42.7 %collective-permute-start.26 = (bf16[96,6912]{1,0:T(8,128)(2,1)}, bf16[96,6912]{1,0:T(8,128)(2,1)S(1)}, u32[]{:S(2)}, u32[]{:S(2)}) collective-permute-start(bf16[96,6912]{1,0:T(8,128)(2,1)} %hold.8.refs_11_.refs_0_.refs_3_), channel_id=1, source_target_pairs={{0,8},{1,9},{2,10},{3,11},{4,12},{5,13},{6,14},{7,15},{8,0},{9,1},... | collective-permute-start | bytes 3981320 | tf_op jit(solution)/shard_map/ppermute | solution.py:1121
  140.4 41.6 %collective-permute-start.27 = (bf16[96,6912]{1,0:T(8,128)(2,1)}, bf16[96,6912]{1,0:T(8,128)(2,1)}, u32[]{:S(2)}, u32[]{:S(2)}) collective-permute-start(bf16[96,6912]{1,0:T(8,128)(2,1)} %hold.8.refs_11_.refs_0_.refs_3_), channel_id=1, source_target_pairs={{0,16},{1,17},{2,18},{3,19},{4,20},{5,21},{6,22},{7,23},{8,24},{9,... | collective-permute-start | bytes 3981320 | tf_op jit(solution)/shard_map/ppermute | solution.py:1121
  189.0 24.2 %collective-permute-start.30 = (bf16[3,96,6912]{2,1,0:T(8,128)(2,1)}, bf16[3,96,6912]{2,1,0:T(8,128)(2,1)}, u32[]{:S(2)}, u32[]{:S(2)}) collective-permute-start(bf16[3,96,6912]{2,1,0:T(8,128)(2,1)} %get-tuple-element.165), channel_id=1, source_target_pairs={{0,4},{1,5},{2,6},{3,7},{4,0},{5,1},{6,2},{7,3},{8,12},{9,13},{10,... | collective-permute-start | bytes 11943944 | tf_op jit(solution)/shard_map/ppermute | solution.py:1121
  264.5 31.1 %collective-permute-start.37 = (bf16[2,96,3072]{2,1,0:T(8,128)(2,1)}, bf16[2,96,3072]{2,1,0:T(8,128)(2,1)S(1)}, u32[]{:S(2)}, u32[]{:S(2)}) collective-permute-start(bf16[2,96,3072]{2,1,0:T(8,128)(2,1)} %get-tuple-element.184.refs_10_), channel_id=1, source_target_pairs={{0,8},{1,9},{2,10},{3,11},{4,12},{5,13},{6,14},{7,15},{8,0},{9,1},... | collective-permute-start | bytes 3538952 | tf_op jit(solution)/shard_map/ppermute | solution.py:1121
  265.6 29.9 %collective-permute-start.38 = (bf16[2,96,3072]{2,1,0:T(8,128)(2,1)}, bf16[2,96,3072]{2,1,0:T(8,128)(2,1)}, u32[]{:S(2)}, u32[]{:S(2)}) collective-permute-start(bf16[2,96,3072]{2,1,0:T(8,128)(2,1)} %get-tuple-element.185.refs_11_), channel_id=1, source_target_pairs={{0,16},{1,17},{2,18},{3,19},{4,20},{5,21},{6,22},{7,23},{8,24},{9,... | collective-permute-start | bytes 3538952 | tf_op jit(solution)/shard_map/ppermute | solution.py:1121
  295.5 24.5 %collective-permute-start.39 = (bf16[4,96,3072]{2,1,0:T(8,128)(2,1)}, bf16[4,96,3072]{2,1,0:T(8,128)(2,1)}, u32[]{:S(2)}, u32[]{:S(2)}) collective-permute-start(bf16[4,96,3072]{2,1,0:T(8,128)(2,1)} %get-tuple-element.201.refs_8_.refs_14_), channel_id=1, source_target_pairs={{0,4},{1,5},{2,6},{3,7},{4,0},{5,1},{6,2},{7,3},{8,12},{9,13},{10,... | collective-permute-start | bytes 7077896 | tf_op jit(solution)/shard_map/ppermute | solution.py:1121
  301.0 49.2 %collective-permute-start.40 = (bf16[1,96,3072]{2,1,0:T(8,128)(2,1)}, bf16[1,96,3072]{2,1,0:T(8,128)(2,1)}, u32[]{:S(2)}, u32[]{:S(2)}) collective-permute-start(bf16[1,96,3072]{2,1,0:T(8,128)(2,1)} %get-tuple-element.202.refs_12_), channel_id=1, source_target_pairs={{0,16},{1,17},{2,18},{3,19},{4,20},{5,21},{6,22},{7,23},{8,24},{9,... | collective-permute-start | bytes 1769480 | tf_op jit(solution)/shard_map/ppermute | solution.py:1121
  302.6 48.7 %collective-permute-start.41 = (bf16[1,96,3072]{2,1,0:T(8,128)(2,1)}, bf16[1,96,3072]{2,1,0:T(8,128)(2,1)}, u32[]{:S(2)}, u32[]{:S(2)}) collective-permute-start(bf16[1,96,3072]{2,1,0:T(8,128)(2,1)} %get-tuple-element.203.refs_13_), channel_id=1, source_target_pairs={{0,8},{1,9},{2,10},{3,11},{4,12},{5,13},{6,14},{7,15},{8,0},{9,1},... | collective-permute-start | bytes 1769480 | tf_op jit(solution)/shard_map/ppermute | solution.py:1121
  324.2 20.3 %collective-permute-start.42 = (bf16[2,96,1536]{2,1,0:T(8,128)(2,1)}, bf16[2,96,1536]{2,1,0:T(8,128)(2,1)S(1)}, u32[]{:S(2)}, u32[]{:S(2)}) collective-permute-start(bf16[2,96,1536]{2,1,0:T(8,128)(2,1)} %get-tuple-element.208.refs_7_), channel_id=1, source_target_pairs={{0,8},{1,9},{2,10},{3,11},{4,12},{5,13},{6,14},{7,15},{8,0},{9,1},... | collective-permute-start | bytes 1769480 | tf_op jit(solution)/shard_map/ppermute | solution.py:1121
  325.4 20.7 %collective-permute-start.43 = (bf16[2,96,1536]{2,1,0:T(8,128)(2,1)}, bf16[2,96,1536]{2,1,0:T(8,128)(2,1)}, u32[]{:S(2)}, u32[]{:S(2)}) collective-permute-start(bf16[2,96,1536]{2,1,0:T(8,128)(2,1)} %get-tuple-element.209.refs_8_), channel_id=1, source_target_pairs={{0,16},{1,17},{2,18},{3,19},{4,20},{5,21},{6,22},{7,23},{8,24},{9,... | collective-permute-start | bytes 1769480 | tf_op jit(solution)/shard_map/ppermute | solution.py:1121
  343.5 29.1 %collective-permute-start.46 = (bf16[2,96,3072]{2,1,0:T(8,128)(2,1)}, bf16[2,96,3072]{2,1,0:T(8,128)(2,1)S(1)}, u32[]{:S(2)}, u32[]{:S(2)}) collective-permute-start(bf16[2,96,3072]{2,1,0:T(8,128)(2,1)} %get-tuple-element.221.refs_8_.refs_6_), channel_id=1, source_target_pairs={{0,8},{1,9},{2,10},{3,11},{4,12},{5,13},{6,14},{7,15},{8,0},{9,1},... | collective-permute-start | bytes 3538952 | tf_op jit(solution)/shard_map/ppermute | solution.py:1121
  344.5 29.2 %collective-permute-start.47 = (bf16[2,96,3072]{2,1,0:T(8,128)(2,1)}, bf16[2,96,3072]{2,1,0:T(8,128)(2,1)}, u32[]{:S(2)}, u32[]{:S(2)}) collective-permute-start(bf16[2,96,3072]{2,1,0:T(8,128)(2,1)} %get-tuple-element.222.refs_9_), channel_id=1, source_target_pairs={{0,16},{1,17},{2,18},{3,19},{4,20},{5,21},{6,22},{7,23},{8,24},{9,... | collective-permute-start | bytes 3538952 | tf_op jit(solution)/shard_map/ppermute | solution.py:1121
  349.4 31.3 %collective-permute-start.50 = (bf16[1,96,1536]{2,1,0:T(8,128)(2,1)}, bf16[1,96,1536]{2,1,0:T(8,128)(2,1)S(1)}, u32[]{:S(2)}, u32[]{:S(2)}) collective-permute-start(bf16[1,96,1536]{2,1,0:T(8,128)(2,1)} %get-tuple-element.223.refs_4_.refs_15_), channel_id=1, source_target_pairs={{0,16},{1,17},{2,18},{3,19},{4,20},{5,21},{6,22},{7,23},{8,24},{9,... | collective-permute-start | bytes 884744 | tf_op jit(solution)/shard_map/ppermute | solution.py:1121
  350.2 30.4 %collective-permute-start.51 = (bf16[1,96,1536]{2,1,0:T(8,128)(2,1)}, bf16[1,96,1536]{2,1,0:T(8,128)(2,1)S(1)}, u32[]{:S(2)}, u32[]{:S(2)}) collective-permute-start(bf16[1,96,1536]{2,1,0:T(8,128)(2,1)} %get-tuple-element.224.refs_5_), channel_id=1, source_target_pairs={{0,8},{1,9},{2,10},{3,11},{4,12},{5,13},{6,14},{7,15},{8,0},{9,1},... | collective-permute-start | bytes 884744 | tf_op jit(solution)/shard_map/ppermute | solution.py:1121
  405.1 28.3 %collective-permute-start.60 = (bf16[2,24,6144]{2,1,0:T(8,128)(2,1)}, bf16[2,24,6144]{2,1,0:T(8,128)(2,1)}, u32[]{:S(2)}, u32[]{:S(2)}) collective-permute-start(bf16[2,24,6144]{2,1,0:T(8,128)(2,1)} %get-tuple-element.246.refs_2_), channel_id=1, source_target_pairs={{0,1},{1,0},{2,3},{3,2},{4,5},{5,4},{6,7},{7,6},{8,9},{9,8},{10,11... | collective-permute-start | bytes 1769480 | tf_op jit(solution)/shard_map/ppermute | solution.py:1121
  432.6 32.3 %collective-permute-start.55 = (bf16[256,768]{1,0:T(8,128)(2,1)S(1)}, bf16[256,768]{1,0:T(8,128)(2,1)S(1)}, u32[]{:S(2)}, u32[]{:S(2)}) collective-permute-start(bf16[256,768]{1,0:T(8,128)(2,1)S(1)} %copy-done.7), channel_id=1, source_target_pairs={{0,0},{4,1},{1,2},{5,3},{2,4},{6,5},{3,6},{7,7},{8,8},{12,9},{9,10... | collective-permute-start | bytes 1179656 | tf_op jit(solution)/shard_map/ppermute | solution.py:1415
  442.5 19.9 %collective-permute-start.61 = (bf16[2,24,3328]{2,1,0:T(8,128)(2,1)}, bf16[2,24,3328]{2,1,0:T(8,128)(2,1)S(1)}, u32[]{:S(2)}, u32[]{:S(2)}) collective-permute-start(bf16[2,24,3328]{2,1,0:T(8,128)(2,1)} %get-tuple-element.259.refs_2_), channel_id=1, source_target_pairs={{0,1},{1,0},{2,3},{3,2},{4,5},{5,4},{6,7},{7,6},{8,9},{9,8},{10,11... | collective-permute-start | bytes 958472 | tf_op jit(solution)/shard_map/ppermute | solution.py:1121
  444.2 25.3 %collective-permute-start.64 = (bf16[24,6144]{1,0:T(8,128)(2,1)S(1)}, bf16[24,6144]{1,0:T(8,128)(2,1)S(1)}, u32[]{:S(2)}, u32[]{:S(2)}) collective-permute-start(bf16[24,6144]{1,0:T(8,128)(2,1)S(1)} %copy-done.10), channel_id=1, source_target_pairs={{0,2},{1,3},{2,0},{3,1},{4,6},{5,7},{6,4},{7,5},{8,10},{9,11},{10,... | collective-permute-start | bytes 884744 | tf_op jit(solution)/shard_map/ppermute | solution.py:1121
  (92 other events, 584.3 us)
Sparse Core Ops, SparseCore 0:
  11.2 47.5 all-gather.2
  62.7 39.8 all-gather.4
  354.4 26.6 reduce-scatter.1
